TPU v7x, 32 devices: a whole 2x2x4 slice. The times are simulated.
32 devices in a mesh: grp: 2 (over y), wide: 8 (over z, x), narrow: 2 (over core).
Axes of the slice: x: 2, y: 2, z: 4, core: 2. Of those that a mesh axis runs over, the one named last changes fastest.
Arguments:
- activations: bfloat16 [16, 16384], P(('grp', 'narrow'), 'wide'), parts along dimension 0, may hold values from -6 to 6
- w_query: bfloat16 [16384, 8192], P('wide', 'narrow'), may hold values from -0.046875 to 0.046875
- w_keyval: bfloat16 [16384, 4, 2, 128], P('wide', 'narrow'), may hold values from -0.046875 to 0.046875
- cache_keys: bfloat16 [16, 4, 2048, 128], P(('grp', 'wide'), 'narrow'), parts along dimension 0, as said below
- cache_values: bfloat16 [16, 4, 2048, 128], P(('grp', 'wide'), 'narrow'), parts along dimension 0, may hold values from -6 to 6
- lengths: int32 [16], P(('grp', 'wide')), parts along dimension 0, may hold values from 1 to 2048, as said below
- w_out: bfloat16 [8192, 16384], P('narrow', 'wide'), may hold values from -0.5 to 0.5
Outputs:
- attention_out: bfloat16 [16, 16384], P(('grp', 'narrow'), 'wide'), parts along dimension 0
There are 2 independent parts, one for each index of `grp`. A program takes and returns all parts, laid end to end along the dimension named above; an argument that names none is the same for every part. Nothing has to cross between parts.
Inputs may be any that keep to these rules, and one draw needn't show every extreme that they name: `lengths`: each sequence holds 1 to 2048 cached tokens; in every draw some sequence holds exactly 2048. `cache_keys`: cached keys are finite.
All inputs are finite; a program needn't handle non-finite values.
Results may differ from a plain program's by a relative error of at most 0.0076.
Values may be sent and summed in bfloat16 or wider, within the bound.
No kernel may reach another device: no remote copies, remote signals or barrier semaphores. Data moves between devices by JAX's collectives and lax.ppermute only.
A program may use at most 128 MiB of HBM per device.

v0:
```python
import math

import jax
import jax.numpy as jnp
from jax import lax
from jax.sharding import PartitionSpec as P

HD = 128


rope_base = 500000.0


def rotate(values, positions):
    half_width = values.shape[-1] // 2
    frequency = rope_base ** (-jnp.arange(half_width, dtype=jnp.float32) / half_width)
    angles = positions.astype(jnp.float32)[:, None] * frequency[None, :]
    cosine = jnp.cos(angles)[:, None, :]
    sine = jnp.sin(angles)[:, None, :]
    front_half = values[..., :half_width]
    back_half = values[..., half_width:]
    return jnp.concatenate(
        [front_half * cosine - back_half * sine, back_half * cosine + front_half * sine], axis=-1
    )


def attend(grouped, new_key, new_value, key_rows, value_rows, lengths):
    score_scale = 1.0 / math.sqrt(grouped.shape[-1])
    scores = (
        jnp.einsum("skgd,sktd->skgt", grouped, key_rows, preferred_element_type=jnp.float32)
        * score_scale
    )
    own_score = (
        jnp.einsum("skgd,skd->skg", grouped, new_key, preferred_element_type=jnp.float32)
        * score_scale
    )
    slots = jnp.arange(key_rows.shape[2], dtype=jnp.int32)
    visible = slots[None, None, None, :] < lengths[:, None, None, None]
    scores = jnp.where(visible, scores, jnp.float32(-1e30))
    row_max = jnp.maximum(jnp.max(scores, axis=-1), own_score)
    weights = jnp.where(visible, jnp.exp(scores - row_max[..., None]), jnp.float32(0.0))
    own_weight = jnp.exp(own_score - row_max)
    denominator = jnp.sum(weights, axis=-1) + own_weight
    probabilities = (weights / denominator[..., None]).astype(jnp.bfloat16)
    own_prob = (own_weight / denominator).astype(jnp.bfloat16)
    attended = jnp.einsum(
        "skgt,sktd->skgd", probabilities, value_rows, preferred_element_type=jnp.float32
    )
    attended = (
        attended
        + own_prob.astype(jnp.float32)[..., None] * new_value.astype(jnp.float32)[:, :, None, :]
    )
    return attended.astype(jnp.bfloat16)


def local(activations, w_query, w_keyval, cache_keys, cache_values, lengths, w_out):
    all_rows = lax.all_gather(activations, "narrow", axis=0, tiled=True)
    wide_count = lax.axis_size("wide")
    seq_local = all_rows.shape[0] // wide_count
    local_kv = cache_keys.shape[1]
    query_cols = w_query.shape[1]
    local_heads = query_cols // HD
    group_size = local_heads // local_kv
    keyval_flat = w_keyval.reshape(w_keyval.shape[0], local_kv * 2 * HD)
    token_block = all_rows
    key_value = lax.psum_scatter(
        jnp.dot(token_block, keyval_flat, preferred_element_type=jnp.float32),
        "wide",
        scatter_dimension=0,
        tiled=True,
    )
    token_block = all_rows
    queries = lax.psum_scatter(
        jnp.dot(token_block, w_query, preferred_element_type=jnp.float32),
        "wide",
        scatter_dimension=0,
        tiled=True,
    )
    queries = queries.reshape(seq_local, local_heads, HD)
    key_value = key_value.reshape(seq_local, local_kv, 2, HD)
    rotated = (
        rotate(queries, lengths).astype(jnp.bfloat16).reshape(seq_local, local_kv, group_size, HD)
    )
    new_key = rotate(key_value[:, :, 0], lengths).astype(jnp.bfloat16)
    new_value = key_value[:, :, 1].astype(jnp.bfloat16)
    attended = attend(rotated, new_key, new_value, cache_keys, cache_values, lengths)
    flat = attended.reshape(seq_local, local_heads * HD)
    partial_out = jnp.dot(
        lax.all_gather(flat, "wide", axis=0, tiled=True), w_out, preferred_element_type=jnp.float32
    )
    summed_out = lax.psum_scatter(partial_out, "narrow", scatter_dimension=0, tiled=True)
    return summed_out.astype(jnp.bfloat16)


def solution(mesh):
    placed = (
        P(("grp", "narrow"), "wide"),
        P("wide", "narrow"),
        P("wide", "narrow", None, None),
        P(("grp", "wide"), "narrow", None, None),
        P(("grp", "wide"), "narrow", None, None),
        P(("grp", "wide")),
        P("narrow", "wide"),
    )
    return jax.shard_map(
        local, mesh=mesh, in_specs=placed, out_specs=P(("grp", "narrow"), "wide"), check_vma=False
    )
```

profile of v0, /device:TPU:0, one launch (start us, length us, event | category | flops | bytes accessed | tf_op | source)
XLA Modules:
  0.0 143.9 jit_solution(8765401299441022177)
XLA Ops:
  6.5 0.0 copy-start
  6.5 0.0 copy-start.2
  6.5 0.0 copy-start.1
  6.5 0.0 all-reduce.5.cloned.1.call-start
  6.5 2.3 %all-gather = bf16[2,4,2048]{2,1,0:T(4,128)(2,1)S(1)} all-gather(bf16[1,4,2048]{2,1,0:T(4,128)(2,1)} %bitcast.47), channel_id=1, replica_groups=mesh['grp'=2,'wide'=8,'narrow'=2] {'narrow'}, dimensions={0}, use_global_device_ids=true | all-gather | bytes 49152 | tf_op jit(solution)/shard_map/all_gather | solution.py:57
  8.9 8.7 %fusion.26 = f32[8,4096]{1,0:T(8,128)} fusion(bf16[8,2048]{1,0:T(8,128)(2,1)S(1)} %reshape.150, bf16[2048,4096]{1,0:T(8,128)(2,1)} %param.8), kind=kOutput, calls=%fused_computation.46 | convolution fusion | flops 134217728 | bytes 16941056 | tf_op jit(solution)/shard_map/dot_general | solution.py:74
  17.6 0.0 all-reduce.5.cloned.1.call-update
  17.6 2.8 %reshape.144 = bf16[2048,512]{1,0:T(8,128)(2,1)S(1)} reshape(bf16[2048,2,2,128]{3,2,1,0:T(2,128)(2,1)} %param.9) | data formatting | bytes 4194304 | tf_op jit(solution)/shard_map/reshape | solution.py:64
  20.3 0.4 fusion.27
  20.7 38.7 %all-reduce.1 = f32[8,512]{1,0:T(8,128)S(1)} all-reduce(f32[8,512]{1,0:T(8,128)S(1)} %fusion.27), channel_id=3, replica_groups=mesh['grp'=2,'wide'=8,'narrow'=2] {'wide'}, use_global_device_ids=true, to_apply=%region_2.3.clone | all-reduce | flops 4096 | bytes 32768
  59.4 0.0 copy-done.2
  59.4 0.6 dynamic-slice
  60.0 0.7 constant_dynamic-slice_fusion
  61.4 0.1 fusion.17
  61.5 0.1 maximum_bitcast_fusion
  61.6 0.0 copy-done.1
  61.6 0.6 dynamic-slice.4
  62.8 27.2 %all-reduce.5.cloned.1.call-done = f32[8,4096]{1,0:T(8,128)} async-done(((f32[8,4096]{1,0:T(8,128)}), f32[8,4096]{1,0:T(8,128)}) %all-reduce.5.cloned.1.call-update) | async-done | bytes 131088
  90.0 1.6 %constant_dynamic-slice_fusion.1 = f32[1,4096]{1,0:T(1,128)S(1)} fusion(f32[8,4096]{1,0:T(8,128)} %all-reduce.5.cloned.1.call-done, u32[]{:T(128)} %bitcast.16), kind=kLoop, calls=%fused_computation.25 | loop fusion | bytes 32772
  91.6 0.1 subtract_convert_fusion
  91.7 0.2 fusion.12
  91.9 0.0 copy-done
  91.9 0.5 fusion.25
  92.4 0.2 fusion.4
  92.6 1.6 %fusion.1 = bf16[2,16,128]{2,1,0:T(8,128)(2,1)S(1)} fusion(bf16[1,2,2048,128]{3,2,1,0:T(8,128)(2,1)} %param.11, f32[2,16,2048]{2,1,0:T(8,128)S(1)} %get-tuple-element.12, f32[2,16]{1,0:T(2,128)S(1)} %get-tuple-element.8, f32[2,16]{1,0:T(2,128)S(1)} %multiply_maximum_fusion, pred[2048]{0:T(1024)(128)(4,1)S(1)} %iota_compare_fusion, f32[2,128]{1,0:T(2,128)S(1)} %fusion.15, ...), kind=kOutput, calls=%fused_computation.3 | convolution fusion | flops 17051648 | bytes 1322368 | tf_op jit(solution)/shard_map/skgt,sktd->skgd/dot_general | solution.py:46
  94.2 30.6 %all-gather.1 = bf16[8,1,4096]{2,1,0:T(2,128)(2,1)S(1)} all-gather(bf16[1,1,4096]{2,1,0:T(2,128)(2,1)S(1)} %reshape.151), channel_id=1, replica_groups=mesh['grp'=2,'wide'=8,'narrow'=2] {'wide'}, dimensions={0}, use_global_device_ids=true | all-gather | bytes 73728 | tf_op jit(solution)/shard_map/all_gather | solution.py:89
  124.8 8.1 %fusion.9 = f32[8,2048]{1,0:T(8,128)S(1)} fusion(bf16[4096,2048]{1,0:T(8,128)(2,1)} %param.13, bf16[8,1,4096]{2,1,0:T(2,128)(2,1)S(1)} %all-gather.1), kind=kOutput, calls=%fused_computation.13 | convolution fusion | flops 134217728 | bytes 16908288 | tf_op jit(solution)/shard_map/dot_general | solution.py:88
  132.8 3.6 %all-reduce.2 = bf16[8,2048]{1,0:T(8,128)(2,1)S(1)} all-reduce(f32[8,2048]{1,0:T(8,128)S(1)} %fusion.9), channel_id=4, replica_groups=mesh['grp'=2,'wide'=8,'narrow'=2] {'narrow'}, use_global_device_ids=true, to_apply=%region_4.5.clone | all-reduce | flops 16384 | bytes 98304
  136.4 0.6 dynamic-slice_convert_fusion
  (10 shorter events, 0.1 us)
Async XLA Ops:
  6.5 85.4 %copy-start = (bf16[1,2,2048,128]{3,2,1,0:T(8,128)(2,1)S(1)}, bf16[1,2,2048,128]{3,2,1,0:T(8,128)(2,1)}, u32[]{:S(2)}) copy-start(bf16[1,2,2048,128]{3,2,1,0:T(8,128)(2,1)} %param.10) | copy-start | bytes 3145732
  6.5 52.9 %copy-start.2 = (u32[32]{0:T(128)S(1)}, u32[32]{0:T(128)}, u32[]{:S(2)}) copy-start(u32[32]{0:T(128)} %constant.19) | copy-start | bytes 388
  6.5 55.0 %copy-start.1 = (u32[32]{0:T(128)S(1)}, u32[32]{0:T(128)}, u32[]{:S(2)}) copy-start(u32[32]{0:T(128)} %constant.27) | copy-start | bytes 388
  6.5 83.5 %all-reduce.5.cloned.1.call-start = ((), (), s32[]{:S(2)}) async-start(), calls=%async_computation | async-start | bytes 262144
Sparse Core Ops, SparseCore 0:
  17.7 72.3 all-reduce.4
where the time goes:
time: 144 us
  blocking collectives  75.2 us (52%)
  waiting for transfers between devices  27.2 us (19%)
  matrix products  19.4 us (13%)
  between operations  14.8 us (10%)
  local copies, waits for them, and re-layouts  6.82 us (5%)
    unnamed x2, blocking collectives  42.3 us
    all_gather x1, blocking collectives, local(): lax.all_gather(flat, 'wide', axis=0, tiled=True)  30.6 us
    unnamed x2, waiting for transfers between devices  27.2 us
    dot_general x1, matrix products, local(): jnp.dot(token_block, w_query, preferred_element_type=jnp.float32)  8.7 us
    dot_general x1, matrix products, local(): jnp.dot(lax.all_gather(flat, 'wide', axis=0, tiled=True), w_out, preferre...  8.05 us
    unnamed x13, local copies, waits for them, and re-layouts  3.44 us
  transfers between devices with their start and end apart: 1, of which 1 were waited for; matrix products, arithmetic and copies ran while one was open for 4% of the time, Pallas kernels for 0%

commit v1 on v0

v1 whole, which is shorter than its diff:
```python
import functools
import math

import jax
import jax.numpy as jnp
from jax import lax
from jax.experimental import pallas as pl
from jax.experimental.pallas import tpu as pltpu
from jax.sharding import PartitionSpec as P

HD = 128
ROPE_BASE = 500000.0
MIB = 2**20
F32, BF16 = jnp.float32, jnp.bfloat16
VMEM = pl.BlockSpec(memory_space=pltpu.VMEM)
SMEM = pl.BlockSpec(memory_space=pltpu.SMEM)
ANY = pl.BlockSpec(memory_space=pl.ANY)


def project_kernel(chunks, core_ref, own_ref, other_ref, w_ref, kv_ref, out_ref, w, kv, sems):
    depth, cols = w_ref.shape
    width = cols // chunks
    kv_copy = pltpu.make_async_copy(kv_ref, kv, sems.at[chunks])
    kv_copy.start()
    copies = []
    for c in range(chunks):
        span = pl.ds(c * width, width)
        copies.append(pltpu.make_async_copy(w_ref.at[:, span], w.at[:, span], sems.at[c]))
        copies[-1].start()

    own, other = own_ref[...].astype(F32), other_ref[...].astype(F32)
    first = core_ref[0] == 0
    wide_rows = jnp.where(
        first, jnp.concatenate([own, other], axis=0), jnp.concatenate([other, own], axis=0)
    )
    rows = wide_rows.astype(BF16)
    count = rows.shape[0]
    heads = cols // HD

    parts = kv_ref.shape[0] // depth
    tiles = depth // HD
    stacked = jnp.concatenate(
        [wide_rows[:, t * HD : (t + 1) * HD] for t in range(tiles)], axis=0
    ).astype(BF16)
    spread_of = lax.broadcasted_iota(jnp.int32, (HD, parts * HD), 0)
    spread_to = lax.broadcasted_iota(jnp.int32, (HD, parts * HD), 1)
    spread = jnp.where(spread_to // parts == spread_of, 1.0, 0.0).astype(BF16)
    repeated = jnp.dot(stacked, spread, preferred_element_type=F32)
    slot = lax.broadcasted_iota(jnp.int32, (count, parts * HD), 1) % parts
    kv_copy.wait()
    total = None
    for t in range(tiles):
        block = repeated[t * count : (t + 1) * count]
        left = jnp.concatenate(
            [jnp.where(slot == p, block, 0.0) for p in range(parts)], axis=0
        ).astype(BF16)
        part = jnp.dot(
            left, kv[t * parts * HD : (t + 1) * parts * HD, :], preferred_element_type=F32
        )
        total = part if total is None else total + part
    for p in range(parts):
        out_ref[:, heads + p, :] = total[p * count : (p + 1) * count]

    for c in range(chunks):
        copies[c].wait()
        block = jnp.dot(rows, w[:, c * width : (c + 1) * width], preferred_element_type=F32)
        for h in range(width // HD):
            out_ref[:, c * (width // HD) + h, :] = block[:, h * HD : (h + 1) * HD]


def attend_kernel(length_ref, cos_ref, sin_ref, parts_ref, keys_ref, values_ref, out_ref):
    summed = parts_ref[0]
    for i in range(1, parts_ref.shape[0]):
        summed = summed + parts_ref[i]
    kv_heads = keys_ref.shape[0]
    heads = parts_ref.shape[1] - 2 * kv_heads
    group = heads // kv_heads
    slots = keys_ref.shape[1]
    rotated = summed * cos_ref[...] + pltpu.roll(summed, HD // 2, 1) * sin_ref[...]
    rotated = rotated.astype(BF16)
    scale = 1.0 / math.sqrt(HD)
    length = length_ref[0]
    visible = lax.broadcasted_iota(jnp.int32, (group, slots), 1) < length
    attended = []
    for k in range(kv_heads):
        query = rotated[k * group : (k + 1) * group]
        new_key = rotated[heads + 2 * k : heads + 2 * k + 1].astype(F32)
        new_value = summed[heads + 2 * k + 1 : heads + 2 * k + 2].astype(BF16).astype(F32)
        scores = (
            lax.dot_general(
                query, keys_ref[k], (((1,), (1,)), ((), ())), preferred_element_type=F32
            )
            * scale
        )
        own = jnp.sum(query.astype(F32) * new_key, axis=-1, keepdims=True) * scale
        scores = jnp.where(visible, scores, -1e30)
        top = jnp.maximum(jnp.max(scores, axis=-1, keepdims=True), own)
        weights = jnp.where(visible, jnp.exp(scores - top), 0.0)
        own_weight = jnp.exp(own - top)
        denominator = jnp.sum(weights, axis=-1, keepdims=True) + own_weight
        probabilities = (weights / denominator).astype(BF16)
        own_prob = (own_weight / denominator).astype(BF16).astype(F32)
        result = jnp.dot(probabilities, values_ref[k], preferred_element_type=F32)
        attended.append((result + own_prob * new_value).astype(BF16))
    block = jnp.concatenate(attended, axis=0)
    for i in range(out_ref.shape[0]):
        out_ref[i] = block


def output_kernel(core_ref, flat_ref, w_ref, keep_ref, send_ref):
    depth, cols = w_ref.shape
    count = keep_ref.shape[0] * 2
    heads = depth // HD
    size = 8 * heads
    to = lax.broadcasted_iota(jnp.int32, (size, size), 0)
    come = lax.broadcasted_iota(jnp.int32, (size, size), 1)
    order = jnp.where((to % 8) * heads + to // 8 == come, 1.0, 0.0).astype(BF16)
    groups = [
        jnp.dot(order, flat_ref[g * size : (g + 1) * size, :], preferred_element_type=F32)
        for g in range(count // 8)
    ]
    left = jnp.concatenate(
        [
            jnp.concatenate([part[h * 8 : (h + 1) * 8] for part in groups], axis=0)
            for h in range(heads)
        ],
        axis=1,
    ).astype(BF16)
    half = count // 2
    first = core_ref[0] == 0
    width = 256
    for c in range(cols // width):
        span = slice(c * width, (c + 1) * width)
        part = jnp.dot(left, w_ref[:, span], preferred_element_type=F32)
        low, high = part[:half, :], part[half:, :]
        keep_ref[:, span] = jnp.where(first, low, high)
        send_ref[:, span] = jnp.where(first, high, low)


def local(activations, w_query, w_keyval, cache_keys, cache_values, lengths, w_out):
    receivers = lax.axis_size("wide")
    core = lax.axis_index("narrow").astype(jnp.int32).reshape(1)
    swap = [(0, 1), (1, 0)]
    rows = activations.shape[0] * 2
    depth, cols = w_query.shape
    kv_heads = w_keyval.shape[1]
    heads = cols // HD
    out_cols = w_out.shape[1]
    half_width = HD // 2

    frequency = ROPE_BASE ** (-jnp.arange(half_width, dtype=F32) / half_width)
    angles = lengths.astype(F32)[:, None] * frequency[None, :]
    cosine, sine = jnp.cos(angles), jnp.sin(angles)
    cosine = jnp.concatenate([cosine, cosine], axis=-1)
    sine = jnp.concatenate([-sine, sine], axis=-1)

    other = lax.ppermute(activations, "narrow", swap)
    q_chunks = 8
    kv_rows = w_keyval.reshape(depth * kv_heads * 2, HD)
    partial = pl.pallas_call(
        functools.partial(project_kernel, q_chunks),
        out_shape=jax.ShapeDtypeStruct((rows, heads + 2 * kv_heads, HD), F32),
        in_specs=[SMEM, VMEM, VMEM, ANY, ANY],
        out_specs=VMEM,
        scratch_shapes=[
            pltpu.VMEM((depth, cols), BF16),
            pltpu.VMEM(kv_rows.shape, BF16),
            pltpu.SemaphoreType.DMA((q_chunks + 1,)),
        ],
        compiler_params=pltpu.CompilerParams(vmem_limit_bytes=46 * MIB),
        cost_estimate=pl.CostEstimate(
            flops=2 * rows * depth * cols, bytes_accessed=18 * MIB, transcendentals=0
        ),
    )(core, activations, other, w_query, kv_rows)
    parts = lax.all_to_all(partial, "wide", 0, 0, tiled=True)
    attended = pl.pallas_call(
        attend_kernel,
        out_shape=jax.ShapeDtypeStruct((receivers, heads, HD), BF16),
        in_specs=[SMEM, VMEM, VMEM, VMEM, VMEM, VMEM],
        out_specs=VMEM,
        compiler_params=pltpu.CompilerParams(vmem_limit_bytes=8 * MIB),
        cost_estimate=pl.CostEstimate(
            flops=4 * heads * 2048 * HD, bytes_accessed=2 * MIB, transcendentals=heads * 2048
        ),
    )(lengths, cosine, sine, parts, cache_keys[0], cache_values[0])
    gathered = lax.all_to_all(attended, "wide", 0, 0, tiled=True)
    keep, send = pl.pallas_call(
        output_kernel,
        out_shape=[jax.ShapeDtypeStruct((rows // 2, out_cols), F32)] * 2,
        in_specs=[SMEM, VMEM, VMEM],
        out_specs=[VMEM, VMEM],
        compiler_params=pltpu.CompilerParams(vmem_limit_bytes=20 * MIB),
        cost_estimate=pl.CostEstimate(
            flops=2 * rows * heads * HD * out_cols, bytes_accessed=16 * MIB, transcendentals=0
        ),
    )(core, gathered.reshape(rows * heads, HD), w_out)
    return (keep + lax.ppermute(send, "narrow", swap)).astype(BF16)


def solution(mesh):
    placed = (
        P(("grp", "narrow"), "wide"),
        P("wide", "narrow"),
        P("wide", "narrow", None, None),
        P(("grp", "wide"), "narrow", None, None),
        P(("grp", "wide"), "narrow", None, None),
        P(("grp", "wide")),
        P("narrow", "wide"),
    )
    return jax.shard_map(
        local, mesh=mesh, in_specs=placed, out_specs=P(("grp", "narrow"), "wide"), check_vma=False
    )
```

time: 144 us -> 47.3 us (0.33)
  blocking collectives: 75.2 us -> 9.64 us
  matrix products: 19.4 us -> 0 us
  waiting for transfers between devices: 27.2 us -> 9.14 us
  between operations: 14.8 us -> 0.69 us
  Pallas kernels: 0 us -> 10.9 us
  starting transfers between devices: 0.01 us -> 7.61 us
    unnamed x2 -> x0, blocking collectives: 42.3 us -> none
    all_gather x2 -> x0, blocking collectives: 32.8 us -> none  [the longest x1 30.6 us: local(): lax.all_gather(flat, 'wide', axis=0, tiled=True)]
    unnamed x2 -> x0, waiting for transfers between devices: 27.2 us -> none
    dot_general x6 -> x0, matrix products: 19.4 us -> none  [the longest x1 8.7 us: local(): jnp.dot(token_block, w_query, preferred_element_type=jnp.float32)]
    pallas_call x0 -> x3, Pallas kernels: none -> 10.9 us  [the longest x1 7.36 us: local(): pl.pallas_call(functools.partial(project_kernel, q_chunks), out_shape=jax...]
    all_to_all x0 -> x1, blocking collectives: none -> 9.64 us  [local(): gathered = lax.all_to_all(attended, 'wide', 0, 0, tiled=True)]
    all_to_all x0 -> x1, waiting for transfers between devices: none -> 7.59 us  [local(): parts = lax.all_to_all(partial, 'wide', 0, 0, tiled=True)]
    all_to_all x0 -> x1, starting transfers between devices: none -> 7.16 us  [local(): parts = lax.all_to_all(partial, 'wide', 0, 0, tiled=True)]
  transfers between devices with their start and end apart: 1 -> 3, of which waited for: 1 -> 3; matrix products, arithmetic and copies ran while one was open for 4% -> 1% of each run, Pallas kernels for 0% -> 0%
where the time goes in v1:
time: 47.3 us; the launch traced here: 46.9 us
  Pallas kernels  10.9 us (23%)
  blocking collectives  9.64 us (20%)
  waiting for transfers between devices  9.14 us (19%)
  local copies, waits for them, and re-layouts  8.08 us (17%)
  starting transfers between devices  7.61 us (16%)
  other arithmetic  0.87 us (2%)
  between operations  0.69 us (1%)
    all_to_all x1, blocking collectives, local(): gathered = lax.all_to_all(attended, 'wide', 0, 0, tiled=True)  9.64 us
    unnamed x10, local copies, waits for them, and re-layouts  8.08 us
    all_to_all x1, waiting for transfers between devices, local(): parts = lax.all_to_all(partial, 'wide', 0, 0, tiled=True)  7.59 us
    pallas_call x1, Pallas kernels, local(): pl.pallas_call(functools.partial(project_kernel, q_chunks), out_shape=jax...  7.36 us
    all_to_all x1, starting transfers between devices, local(): parts = lax.all_to_all(partial, 'wide', 0, 0, tiled=True)  7.16 us
    pallas_call x1, Pallas kernels, local(): pl.pallas_call(output_kernel, out_shape=[jax.ShapeDtypeStruct((rows // 2,...  2.38 us
    ppermute x1, waiting for transfers between devices, local(): return (keep + lax.ppermute(send, 'narrow', swap)).astype(BF16)  1.21 us
    pallas_call x1, Pallas kernels, local(): pl.pallas_call(attend_kernel, out_shape=jax.ShapeDtypeStruct((receivers,...  1.15 us
  transfers between devices with their start and end apart: 3, of which 3 were waited for; matrix products, arithmetic and copies ran while one was open for 1% of the time, Pallas kernels for 0%

profile of v1, /device:TPU:0, one launch (start us, length us, event | category | flops | bytes accessed | tf_op | source)
XLA Modules:
  0.0 46.9 jit_solution(15775849519165235654)
XLA Ops:
  0.0 0.5 collective-permute-start
  1.1 0.1 fusion
  1.2 0.3 collective-permute-done.other_ref
  1.5 0.0 copy-start.1
  1.5 1.6 %copy-done.1 = bf16[2048,2,2,128]{3,2,1,0:T(2,128)(2,1)S(1)} copy-done((bf16[2048,2,2,128]{3,2,1,0:T(2,128)(2,1)S(1)}, bf16[2048,2,2,128]{3,2,1,0:T(2,128)(2,1)}, u32[]{:S(2)}) %copy-start.1) | copy-done | bytes 2097176
  3.1 0.0 copy-start.4
  3.1 0.7 %copy-done.4 = bf16[4,2048]{1,0:T(4,128)(2,1)S(1)} copy-done((bf16[4,2048]{1,0:T(4,128)(2,1)S(1)}, bf16[4,2048]{1,0:T(4,128)(2,1)}, u32[]{:S(2)}) %copy-start.4) | copy-done | bytes 16408
  3.8 0.0 copy-start.2
  3.8 0.0 copy-start.3
  3.8 7.4 %shard_map.73 = f32[8,36,128]{2,1,0:T(8,128)} custom-call(s32[1]{0:T(128)} %bitcast.core_ref, bf16[4,2048]{1,0:T(4,128)(2,1)S(1)} %copy-done.4, bf16[4,2048]{1,0:T(4,128)(2,1)S(1)} %collective-permute-done.other_ref, bf16[2048,4096]{1,0:T(8,128)(2,1)} %w_ref.2, bf16[8192,128]{1,0:T(8,128)(2,1)S(1)} %bitcast.6), custom_call_target="tpu_custom_call" | custom-call | flops 134217728 | bytes 18874368 | tf_op jit(solution)/shard_map/pallas_call | solution.py:160
  11.2 7.2 %all-to-all-start = ((f32[8,36,128]{2,1,0:T(8,128)}), f32[8,36,128]{2,1,0:T(8,128)S(1)}, u32[]{:S(2)}, u32[]{:S(2)}) async-start(f32[8,36,128]{2,1,0:T(8,128)} %shard_map.73), calls=%async_computation | async-start | bytes 327680 | tf_op jit(solution)/shard_map/all_to_all | solution.py:175
  18.3 0.1 fusion.2
  18.4 0.1 pad_maximum_fusion.cos_ref
  18.5 0.1 pad_maximum_fusion.1.sin_ref
  18.6 7.6 %all-to-all-done.parts_ref = f32[8,36,128]{2,1,0:T(8,128)S(1)} async-done(((f32[8,36,128]{2,1,0:T(8,128)}), f32[8,36,128]{2,1,0:T(8,128)S(1)}, u32[]{:S(2)}, u32[]{:S(2)}) %all-to-all-start) | async-done | bytes 147488 | tf_op jit(solution)/shard_map/all_to_all | solution.py:175
  26.1 0.0 copy-done.2
  26.1 0.0 copy-done.3
  26.1 1.2 %shard_map.74 = bf16[8,32,128]{2,1,0:T(8,128)(2,1)S(1)} custom-call(s32[1]{0:T(128)S(6)} %copy.8.length_ref, f32[1,128]{1,0:T(1,128)S(1)} %pad_maximum_fusion.cos_ref, f32[1,128]{1,0:T(1,128)S(1)} %pad_maximum_fusion.1.sin_ref, f32[8,36,128]{2,1,0:T(8,128)S(1)} %all-to-all-done.parts_ref, bf16[2,2048,128]{2,1,0:T(8,128)(2,1)S(1)} %bitcast.7, ...), custom_call_target="tpu_custom_call" | custom-call | flops 33554432 | bytes 2097152 | tf_op jit(solution)/shard_map/pallas_call | solution.py:176
  27.3 9.6 %all_to_all.10 = bf16[8,32,128]{2,1,0:T(8,128)(2,1)S(1)} all-to-all(bf16[8,32,128]{2,1,0:T(8,128)(2,1)S(1)} %shard_map.74), channel_id=1, replica_groups=mesh['grp'=2,'wide'=8,'narrow'=2] {'wide'}, dimensions={0} | all-to-all | bytes 131072 | tf_op jit(solution)/shard_map/all_to_all | solution.py:186
  36.9 0.0 copy-start
  36.9 5.8 %copy-done = bf16[4096,2048]{1,0:T(8,128)(2,1)S(1)} copy-done((bf16[4096,2048]{1,0:T(8,128)(2,1)S(1)}, bf16[4096,2048]{1,0:T(8,128)(2,1)}, u32[]{:S(2)}) %copy-start) | copy-done | bytes 16777240
  42.7 2.4 %shard_map.75 = (f32[4,2048]{1,0:T(4,128)S(1)}, f32[4,2048]{1,0:T(4,128)S(1)}) custom-call(s32[1]{0:T(128)} %bitcast.core_ref, bf16[256,128]{1,0:T(8,128)(2,1)S(1)} %bitcast.9, bf16[4096,2048]{1,0:T(8,128)(2,1)S(1)} %copy-done), custom_call_target="tpu_custom_call" | custom-call | flops 134217728 | bytes 16777216 | tf_op jit(solution)/shard_map/pallas_call | solution.py:187
  45.1 0.0 collective-permute-start.1
  45.1 1.2 %collective-permute-done.1 = f32[4,2048]{1,0:T(4,128)S(1)} collective-permute-done((f32[4,2048]{1,0:T(4,128)S(1)}, f32[4,2048]{1,0:T(4,128)S(1)}, u32[]{:S(2)}, u32[]{:S(2)}) %collective-permute-start.1) | collective-permute-done | bytes 32800 | tf_op jit(solution)/shard_map/ppermute | solution.py:197
  46.3 0.6 %add_convert_fusion = bf16[4,2048]{1,0:T(4,128)(2,1)} fusion(f32[4,2048]{1,0:T(4,128)S(1)} %get-tuple-element.7, f32[4,2048]{1,0:T(4,128)S(1)} %collective-permute-done.1), kind=kLoop, calls=%fused_computation | loop fusion | flops 16384 | bytes 81920 | tf_op jit(solution)/shard_map/convert_element_type | solution.py:197
Async XLA Ops:
  0.0 1.5 %collective-permute-start = (bf16[4,2048]{1,0:T(4,128)(2,1)}, bf16[4,2048]{1,0:T(4,128)(2,1)S(1)}, u32[]{:S(2)}, u32[]{:S(2)}) collective-permute-start(bf16[4,2048]{1,0:T(4,128)(2,1)} %own_ref.1), channel_id=1, source_target_pairs={{0,1},{1,0},{2,3},{3,2},{4,5},{5,4},{6,7},{7,6},{8,9},{9,8},{10,11... | collective-permute-start | bytes 49160 | tf_op jit(solution)/shard_map/ppermute | solution.py:157
  1.5 1.6 %copy-start.1 = (bf16[2048,2,2,128]{3,2,1,0:T(2,128)(2,1)S(1)}, bf16[2048,2,2,128]{3,2,1,0:T(2,128)(2,1)}, u32[]{:S(2)}) copy-start(bf16[2048,2,2,128]{3,2,1,0:T(2,128)(2,1)} %param.9) | copy-start | bytes 6291460
  3.1 0.7 %copy-start.4 = (bf16[4,2048]{1,0:T(4,128)(2,1)S(1)}, bf16[4,2048]{1,0:T(4,128)(2,1)}, u32[]{:S(2)}) copy-start(bf16[4,2048]{1,0:T(4,128)(2,1)} %own_ref.1) | copy-start | bytes 49156
  3.8 22.3 %copy-start.2 = (bf16[1,2,2048,128]{3,2,1,0:T(8,128)(2,1)S(1)}, bf16[1,2,2048,128]{3,2,1,0:T(8,128)(2,1)}, u32[]{:S(2)}) copy-start(bf16[1,2,2048,128]{3,2,1,0:T(8,128)(2,1)} %param.10) | copy-start | bytes 3145732
  3.8 22.3 %copy-start.3 = (bf16[1,2,2048,128]{3,2,1,0:T(8,128)(2,1)S(1)}, bf16[1,2,2048,128]{3,2,1,0:T(8,128)(2,1)}, u32[]{:S(2)}) copy-start(bf16[1,2,2048,128]{3,2,1,0:T(8,128)(2,1)} %param.11) | copy-start | bytes 3145732
  11.2 15.0 %all-to-all-start = ((f32[8,36,128]{2,1,0:T(8,128)}), f32[8,36,128]{2,1,0:T(8,128)S(1)}, u32[]{:S(2)}, u32[]{:S(2)}) async-start(f32[8,36,128]{2,1,0:T(8,128)} %shard_map.73), calls=%async_computation | async-start | bytes 327680 | tf_op jit(solution)/shard_map/all_to_all | solution.py:175
  36.9 5.8 %copy-start = (bf16[4096,2048]{1,0:T(8,128)(2,1)S(1)}, bf16[4096,2048]{1,0:T(8,128)(2,1)}, u32[]{:S(2)}) copy-start(bf16[4096,2048]{1,0:T(8,128)(2,1)} %w_ref.3) | copy-start | bytes 50331652
  45.1 1.2 %collective-permute-start.1 = (f32[4,2048]{1,0:T(4,128)S(1)}, f32[4,2048]{1,0:T(4,128)S(1)}, u32[]{:S(2)}, u32[]{:S(2)}) collective-permute-start(f32[4,2048]{1,0:T(4,128)S(1)} %get-tuple-element.8), channel_id=1, source_target_pairs={{0,1},{1,0},{2,3},{3,2},{4,5},{5,4},{6,7},{7,6},{8,9},{9,8},{10,11... | collective-permute-start | bytes 98312 | tf_op jit(solution)/shard_map/ppermute | solution.py:197

commit v2 on v1

--- a/solution.py
+++ b/solution.py
@@ -17,9 +17,19 @@
 ANY = pl.BlockSpec(memory_space=pl.ANY)
 
 
-def project_kernel(chunks, core_ref, own_ref, other_ref, w_ref, kv_ref, out_ref, w, kv, sems):
+def in_hbm(array):
+    return pltpu.with_memory_space_constraint(array, pltpu.HBM)
+
+
+def in_vmem(array):
+    return pltpu.with_memory_space_constraint(array, pltpu.VMEM)
+
+
+def project_kernel(chunks, core_ref, after_ref, own_hbm, other_ref, w_ref, kv_ref, out_ref, own_ref, w, kv, sems):
     depth, cols = w_ref.shape
     width = cols // chunks
+    own_copy = pltpu.make_async_copy(own_hbm, own_ref, sems.at[chunks + 1])
+    own_copy.start()
     kv_copy = pltpu.make_async_copy(kv_ref, kv, sems.at[chunks])
     kv_copy.start()
     copies = []
@@ -28,6 +38,7 @@
         copies.append(pltpu.make_async_copy(w_ref.at[:, span], w.at[:, span], sems.at[c]))
         copies[-1].start()
 
+    own_copy.wait()
     own, other = own_ref[...].astype(F32), other_ref[...].astype(F32)
     first = core_ref[0] == 0
     wide_rows = jnp.where(
@@ -68,7 +79,7 @@
             out_ref[:, c * (width // HD) + h, :] = block[:, h * HD : (h + 1) * HD]
 
 
-def attend_kernel(length_ref, cos_ref, sin_ref, parts_ref, keys_ref, values_ref, out_ref):
+def attend_kernel(length_ref, turns_ref, parts_ref, keys_ref, values_ref, out_ref):
     summed = parts_ref[0]
     for i in range(1, parts_ref.shape[0]):
         summed = summed + parts_ref[i]
@@ -76,7 +87,7 @@
     heads = parts_ref.shape[1] - 2 * kv_heads
     group = heads // kv_heads
     slots = keys_ref.shape[1]
-    rotated = summed * cos_ref[...] + pltpu.roll(summed, HD // 2, 1) * sin_ref[...]
+    rotated = summed * turns_ref[:1] + pltpu.roll(summed, HD // 2, 1) * turns_ref[1:]
     rotated = rotated.astype(BF16)
     scale = 1.0 / math.sqrt(HD)
     length = length_ref[0]
@@ -151,38 +162,38 @@
     frequency = ROPE_BASE ** (-jnp.arange(half_width, dtype=F32) / half_width)
     angles = lengths.astype(F32)[:, None] * frequency[None, :]
     cosine, sine = jnp.cos(angles), jnp.sin(angles)
-    cosine = jnp.concatenate([cosine, cosine], axis=-1)
-    sine = jnp.concatenate([-sine, sine], axis=-1)
+    turns = jnp.concatenate([cosine, cosine, -sine, sine], axis=-1).reshape(2, HD)
 
     other = lax.ppermute(activations, "narrow", swap)
     q_chunks = 8
     kv_rows = w_keyval.reshape(depth * kv_heads * 2, HD)
     partial = pl.pallas_call(
         functools.partial(project_kernel, q_chunks),
-        out_shape=jax.ShapeDtypeStruct((rows, heads + 2 * kv_heads, HD), F32),
-        in_specs=[SMEM, VMEM, VMEM, ANY, ANY],
+        out_shape=pltpu.VMEM((rows, heads + 2 * kv_heads, HD), F32),
+        in_specs=[SMEM, ANY, ANY, VMEM, ANY, ANY],
         out_specs=VMEM,
         scratch_shapes=[
+            pltpu.VMEM(activations.shape, BF16),
             pltpu.VMEM((depth, cols), BF16),
             pltpu.VMEM(kv_rows.shape, BF16),
-            pltpu.SemaphoreType.DMA((q_chunks + 1,)),
+            pltpu.SemaphoreType.DMA((q_chunks + 2,)),
         ],
-        compiler_params=pltpu.CompilerParams(vmem_limit_bytes=46 * MIB),
+        compiler_params=pltpu.CompilerParams(vmem_limit_bytes=24 * MIB),
         cost_estimate=pl.CostEstimate(
             flops=2 * rows * depth * cols, bytes_accessed=18 * MIB, transcendentals=0
         ),
-    )(core, activations, other, w_query, kv_rows)
+    )(core, turns, in_hbm(activations), other, in_hbm(w_query), in_hbm(kv_rows))
     parts = lax.all_to_all(partial, "wide", 0, 0, tiled=True)
     attended = pl.pallas_call(
         attend_kernel,
         out_shape=jax.ShapeDtypeStruct((receivers, heads, HD), BF16),
-        in_specs=[SMEM, VMEM, VMEM, VMEM, VMEM, VMEM],
+        in_specs=[SMEM, VMEM, VMEM, VMEM, VMEM],
         out_specs=VMEM,
         compiler_params=pltpu.CompilerParams(vmem_limit_bytes=8 * MIB),
         cost_estimate=pl.CostEstimate(
             flops=4 * heads * 2048 * HD, bytes_accessed=2 * MIB, transcendentals=heads * 2048
         ),
-    )(lengths, cosine, sine, parts, cache_keys[0], cache_values[0])
+    )(lengths, turns, parts, cache_keys[0], cache_values[0])
     gathered = lax.all_to_all(attended, "wide", 0, 0, tiled=True)
     keep, send = pl.pallas_call(
         output_kernel,
@@ -193,7 +204,7 @@
         cost_estimate=pl.CostEstimate(
             flops=2 * rows * heads * HD * out_cols, bytes_accessed=16 * MIB, transcendentals=0
         ),
-    )(core, gathered.reshape(rows * heads, HD), w_out)
+    )(core, gathered.reshape(rows * heads, HD), in_vmem(w_out))
     return (keep + lax.ppermute(send, "narrow", swap)).astype(BF16)
 
 

time: 47.3 us -> 39 us (0.82)
  blocking collectives: 9.64 us -> 24.6 us
  local copies, waits for them, and re-layouts: 8.08 us -> 0.01 us
  waiting for transfers between devices: 9.14 us -> 1.24 us
  starting transfers between devices: 7.61 us -> 0.46 us
    all_to_all x0 -> x1, blocking collectives: none -> 15 us  [local(): parts = lax.all_to_all(partial, 'wide', 0, 0, tiled=True)]
    unnamed x10 -> x6, local copies, waits for them, and re-layouts: 8.08 us -> 0.01 us
    all_to_all x1 -> x0, waiting for transfers between devices: 7.59 us -> none  [local(): parts = lax.all_to_all(partial, 'wide', 0, 0, tiled=True)]
    all_to_all x1 -> x0, starting transfers between devices: 7.16 us -> none  [local(): parts = lax.all_to_all(partial, 'wide', 0, 0, tiled=True)]
  transfers between devices with their start and end apart: 3 -> 2, of which waited for: 3 -> 1; matrix products, arithmetic and copies ran while one was open for 1% -> 0% of each run, Pallas kernels for 0% -> 0%
where the time goes in v2:
time: 39 us; the launch traced here: 38.7 us
  blocking collectives  24.6 us (63%)
  Pallas kernels  10.7 us (27%)
  waiting for transfers between devices  1.24 us (3%)
  between operations  0.85 us (2%)
  other arithmetic  0.8 us (2%)
  starting transfers between devices  0.46 us (1%)
    all_to_all x1, blocking collectives, local(): parts = lax.all_to_all(partial, 'wide', 0, 0, tiled=True)  15 us
    all_to_all x1, blocking collectives, local(): gathered = lax.all_to_all(attended, 'wide', 0, 0, tiled=True)  9.64 us
    pallas_call x1, Pallas kernels, local(): pl.pallas_call(functools.partial(project_kernel, q_chunks), out_shape=plt...  7.21 us
    pallas_call x1, Pallas kernels, local(): pl.pallas_call(output_kernel, out_shape=[jax.ShapeDtypeStruct((rows // 2,...  2.38 us
    ppermute x1, waiting for transfers between devices, local(): return (keep + lax.ppermute(send, 'narrow', swap)).astype(BF16)  1.21 us
    pallas_call x1, Pallas kernels, local(): pl.pallas_call(attend_kernel, out_shape=jax.ShapeDtypeStruct((receivers,...  1.16 us
  transfers between devices with their start and end apart: 2, of which 1 were waited for; matrix products, arithmetic and copies ran while one was open for 0% of the time, Pallas kernels for 0%

profile of v2, /device:TPU:0, one launch (start us, length us, event | category | flops | bytes accessed | tf_op | source)
XLA Modules:
  0.0 38.7 jit_solution(7183294490493152437)
XLA Ops:
  0.0 0.0 copy-start.2
  0.0 0.0 copy-start.1
  0.0 0.5 %collective-permute-start = (bf16[4,2048]{1,0:T(4,128)(2,1)}, bf16[4,2048]{1,0:T(4,128)(2,1)S(1)}, u32[]{:S(2)}, u32[]{:S(2)}) collective-permute-start(bf16[4,2048]{1,0:T(4,128)(2,1)} %own_hbm.1), channel_id=1, source_target_pairs={{0,1},{1,0},{2,3},{3,2},{4,5},{5,4},{6,7},{7,6},{8,9},{9,8},{10,11... | collective-permute-start | bytes 49160 | tf_op jit(solution)/shard_map/ppermute | solution.py:167
  1.3 0.1 fusion.2
  1.3 0.1 fusion
  1.4 0.1 pad_maximum_fusion
  1.5 0.0 copy-start
  1.5 0.0 collective-permute-done.other_ref
  1.5 7.2 %shard_map.73 = f32[8,36,128]{2,1,0:T(8,128)S(1)} custom-call(s32[1]{0:T(128)} %bitcast.core_ref, f32[2,128]{1,0:T(2,128)S(1)} %bitcast.10, bf16[4,2048]{1,0:T(4,128)(2,1)} %own_hbm.1, bf16[4,2048]{1,0:T(4,128)(2,1)S(1)} %collective-permute-done.other_ref, bf16[2048,4096]{1,0:T(8,128)(2,1)} %w_ref.2, bf16[8192,128]{1,0:T(8,128)(2,1)} %bitcast.12), custom_call_target="tpu_custom_call" | custom-call | flops 134217728 | bytes 18874368 | tf_op jit(solution)/shard_map/pallas_call | solution.py:170
  8.7 15.0 %all_to_all.10.parts_ref = f32[8,36,128]{2,1,0:T(8,128)S(1)} all-to-all(f32[8,36,128]{2,1,0:T(8,128)S(1)} %shard_map.73), channel_id=1, replica_groups=mesh['grp'=2,'wide'=8,'narrow'=2] {'wide'}, dimensions={0} | all-to-all | bytes 294912 | tf_op jit(solution)/shard_map/all_to_all | solution.py:186
  23.7 0.0 copy-done.2
  23.7 0.0 copy-done.1
  23.7 1.2 %shard_map.74 = bf16[8,32,128]{2,1,0:T(8,128)(2,1)S(1)} custom-call(s32[1]{0:T(128)S(6)} %copy.8.length_ref, f32[2,128]{1,0:T(2,128)S(1)} %bitcast.11, f32[8,36,128]{2,1,0:T(8,128)S(1)} %all_to_all.10.parts_ref, bf16[2,2048,128]{2,1,0:T(8,128)(2,1)S(1)} %bitcast.7, bf16[2,2048,128]{2,1,0:T(8,128)(2,1)S(1)} %bitcast.8), custom_call_target="tpu_custom_call" | custom-call | flops 33554432 | bytes 2097152 | tf_op jit(solution)/shard_map/pallas_call | solution.py:187
  24.9 9.6 %all_to_all.11 = bf16[8,32,128]{2,1,0:T(8,128)(2,1)S(1)} all-to-all(bf16[8,32,128]{2,1,0:T(8,128)(2,1)S(1)} %shard_map.74), channel_id=1, replica_groups=mesh['grp'=2,'wide'=8,'narrow'=2] {'wide'}, dimensions={0} | all-to-all | bytes 131072 | tf_op jit(solution)/shard_map/all_to_all | solution.py:197
  34.5 0.0 copy-done
  34.5 2.4 %shard_map.75 = (f32[4,2048]{1,0:T(4,128)S(1)}, f32[4,2048]{1,0:T(4,128)S(1)}) custom-call(s32[1]{0:T(128)} %bitcast.core_ref, bf16[256,128]{1,0:T(8,128)(2,1)S(1)} %bitcast.9, bf16[4096,2048]{1,0:T(8,128)(2,1)S(1)} %copy-done), custom_call_target="tpu_custom_call" | custom-call | flops 134217728 | bytes 16777216 | tf_op jit(solution)/shard_map/pallas_call | solution.py:198
  36.9 0.0 collective-permute-start.1
  36.9 1.2 %collective-permute-done.1 = f32[4,2048]{1,0:T(4,128)S(1)} collective-permute-done((f32[4,2048]{1,0:T(4,128)S(1)}, f32[4,2048]{1,0:T(4,128)S(1)}, u32[]{:S(2)}, u32[]{:S(2)}) %collective-permute-start.1) | collective-permute-done | bytes 32800 | tf_op jit(solution)/shard_map/ppermute | solution.py:208
  38.1 0.6 %add_convert_fusion = bf16[4,2048]{1,0:T(4,128)(2,1)} fusion(f32[4,2048]{1,0:T(4,128)S(1)} %get-tuple-element.7, f32[4,2048]{1,0:T(4,128)S(1)} %collective-permute-done.1), kind=kLoop, calls=%fused_computation | loop fusion | flops 16384 | bytes 81920 | tf_op jit(solution)/shard_map/convert_element_type | solution.py:208
Async XLA Ops:
  0.0 23.7 %copy-start.2 = (bf16[1,2,2048,128]{3,2,1,0:T(8,128)(2,1)S(1)}, bf16[1,2,2048,128]{3,2,1,0:T(8,128)(2,1)}, u32[]{:S(2)}) copy-start(bf16[1,2,2048,128]{3,2,1,0:T(8,128)(2,1)} %param.11) | copy-start | bytes 3145732
  0.0 23.7 %copy-start.1 = (bf16[1,2,2048,128]{3,2,1,0:T(8,128)(2,1)S(1)}, bf16[1,2,2048,128]{3,2,1,0:T(8,128)(2,1)}, u32[]{:S(2)}) copy-start(bf16[1,2,2048,128]{3,2,1,0:T(8,128)(2,1)} %param.10) | copy-start | bytes 3145732
  0.0 1.5 %collective-permute-start = (bf16[4,2048]{1,0:T(4,128)(2,1)}, bf16[4,2048]{1,0:T(4,128)(2,1)S(1)}, u32[]{:S(2)}, u32[]{:S(2)}) collective-permute-start(bf16[4,2048]{1,0:T(4,128)(2,1)} %own_hbm.1), channel_id=1, source_target_pairs={{0,1},{1,0},{2,3},{3,2},{4,5},{5,4},{6,7},{7,6},{8,9},{9,8},{10,11... | collective-permute-start | bytes 49160 | tf_op jit(solution)/shard_map/ppermute | solution.py:167
  1.5 33.1 %copy-start = (bf16[4096,2048]{1,0:T(8,128)(2,1)S(1)}, bf16[4096,2048]{1,0:T(8,128)(2,1)}, u32[]{:S(2)}) copy-start(bf16[4096,2048]{1,0:T(8,128)(2,1)} %w_ref.3) | copy-start | bytes 50331652
  36.9 1.2 %collective-permute-start.1 = (f32[4,2048]{1,0:T(4,128)S(1)}, f32[4,2048]{1,0:T(4,128)S(1)}, u32[]{:S(2)}, u32[]{:S(2)}) collective-permute-start(f32[4,2048]{1,0:T(4,128)S(1)} %get-tuple-element.8), channel_id=1, source_target_pairs={{0,1},{1,0},{2,3},{3,2},{4,5},{5,4},{6,7},{7,6},{8,9},{9,8},{10,11... | collective-permute-start | bytes 98312 | tf_op jit(solution)/shard_map/ppermute | solution.py:208

commit v3 on v2

--- a/solution.py
+++ b/solution.py
@@ -12,6 +12,7 @@
 ROPE_BASE = 500000.0
 MIB = 2**20
 F32, BF16 = jnp.float32, jnp.bfloat16
+SPAN = 7_000_000_000
 VMEM = pl.BlockSpec(memory_space=pltpu.VMEM)
 SMEM = pl.BlockSpec(memory_space=pltpu.SMEM)
 ANY = pl.BlockSpec(memory_space=pl.ANY)
@@ -25,18 +26,26 @@
     return pltpu.with_memory_space_constraint(array, pltpu.VMEM)
 
 
-def project_kernel(chunks, core_ref, after_ref, own_hbm, other_ref, w_ref, kv_ref, out_ref, own_ref, w, kv, sems):
+def turns_kernel(cosine_ref, sine_ref, out_ref):
+    cosine, sine = cosine_ref[...], sine_ref[...]
+    out_ref[...] = jnp.concatenate(
+        [jnp.concatenate([cosine, cosine], axis=1), jnp.concatenate([-sine, sine], axis=1)], axis=0
+    )
+
+
+def project_kernel(
+    heights, core_ref, after_ref, own_hbm, other_ref, w_ref, kv_ref, sums, own_ref, w, held, sems
+):
     depth, cols = w_ref.shape
-    width = cols // chunks
-    own_copy = pltpu.make_async_copy(own_hbm, own_ref, sems.at[chunks + 1])
+    own_copy = pltpu.make_async_copy(own_hbm, own_ref, sems.at[len(heights)])
     own_copy.start()
-    kv_copy = pltpu.make_async_copy(kv_ref, kv, sems.at[chunks])
-    kv_copy.start()
-    copies = []
-    for c in range(chunks):
-        span = pl.ds(c * width, width)
-        copies.append(pltpu.make_async_copy(w_ref.at[:, span], w.at[:, span], sems.at[c]))
+    copies, spans, at = [], [], 0
+    for c, height in enumerate(heights):
+        span = pl.ds(at, height)
+        copies.append(pltpu.make_async_copy(w_ref.at[span], w.at[span], sems.at[c]))
         copies[-1].start()
+        spans.append((at, height))
+        at += height
 
     own_copy.wait()
     own, other = own_ref[...].astype(F32), other_ref[...].astype(F32)
@@ -58,7 +67,6 @@
     spread = jnp.where(spread_to // parts == spread_of, 1.0, 0.0).astype(BF16)
     repeated = jnp.dot(stacked, spread, preferred_element_type=F32)
     slot = lax.broadcasted_iota(jnp.int32, (count, parts * HD), 1) % parts
-    kv_copy.wait()
     total = None
     for t in range(tiles):
         block = repeated[t * count : (t + 1) * count]
@@ -66,17 +74,23 @@
             [jnp.where(slot == p, block, 0.0) for p in range(parts)], axis=0
         ).astype(BF16)
         part = jnp.dot(
-            left, kv[t * parts * HD : (t + 1) * parts * HD, :], preferred_element_type=F32
+            left, kv_ref[t * parts * HD : (t + 1) * parts * HD, :], preferred_element_type=F32
         )
         total = part if total is None else total + part
     for p in range(parts):
-        out_ref[:, heads + p, :] = total[p * count : (p + 1) * count]
-
-    for c in range(chunks):
+        sums[:, heads + p, :] = total[p * count : (p + 1) * count]
+
+    for c, (at, height) in enumerate(spans):
         copies[c].wait()
-        block = jnp.dot(rows, w[:, c * width : (c + 1) * width], preferred_element_type=F32)
-        for h in range(width // HD):
-            out_ref[:, c * (width // HD) + h, :] = block[:, h * HD : (h + 1) * HD]
+        block = jnp.dot(
+            rows[:, at : at + height], w[at : at + height, :], preferred_element_type=F32
+        )
+        if c > 0:
+            block = block + held[...]
+        if c < len(spans) - 1:
+            held[...] = block
+    for h in range(heads):
+        sums[:, h, :] = block[:, h * HD : (h + 1) * HD]
 
 
 def attend_kernel(length_ref, turns_ref, parts_ref, keys_ref, values_ref, out_ref):
@@ -109,8 +123,9 @@
         weights = jnp.where(visible, jnp.exp(scores - top), 0.0)
         own_weight = jnp.exp(own - top)
         denominator = jnp.sum(weights, axis=-1, keepdims=True) + own_weight
-        probabilities = (weights / denominator).astype(BF16)
-        own_prob = (own_weight / denominator).astype(BF16).astype(F32)
+        inverse = 1.0 / denominator
+        probabilities = (weights * inverse).astype(BF16)
+        own_prob = (own_weight * inverse).astype(BF16).astype(F32)
         result = jnp.dot(probabilities, values_ref[k], preferred_element_type=F32)
         attended.append((result + own_prob * new_value).astype(BF16))
     block = jnp.concatenate(attended, axis=0)
@@ -139,7 +154,7 @@
     ).astype(BF16)
     half = count // 2
     first = core_ref[0] == 0
-    width = 256
+    width = 1024
     for c in range(cols // width):
         span = slice(c * width, (c + 1) * width)
         part = jnp.dot(left, w_ref[:, span], preferred_element_type=F32)
@@ -162,27 +177,34 @@
     frequency = ROPE_BASE ** (-jnp.arange(half_width, dtype=F32) / half_width)
     angles = lengths.astype(F32)[:, None] * frequency[None, :]
     cosine, sine = jnp.cos(angles), jnp.sin(angles)
-    turns = jnp.concatenate([cosine, cosine, -sine, sine], axis=-1).reshape(2, HD)
+    turns = pl.pallas_call(
+        turns_kernel,
+        out_shape=jax.ShapeDtypeStruct((2, HD), F32),
+        in_specs=[VMEM, VMEM],
+        out_specs=VMEM,
+        compiler_params=pltpu.CompilerParams(vmem_limit_bytes=MIB),
+        cost_estimate=pl.CostEstimate(flops=SPAN, bytes_accessed=MIB, transcendentals=0),
+    )(cosine, sine)
 
     other = lax.ppermute(activations, "narrow", swap)
-    q_chunks = 8
+    heights = [depth // 8] * 7 + [depth // 16] * 2 if depth % 256 == 0 else [depth]
     kv_rows = w_keyval.reshape(depth * kv_heads * 2, HD)
     partial = pl.pallas_call(
-        functools.partial(project_kernel, q_chunks),
+        functools.partial(project_kernel, heights),
         out_shape=pltpu.VMEM((rows, heads + 2 * kv_heads, HD), F32),
-        in_specs=[SMEM, ANY, ANY, VMEM, ANY, ANY],
+        in_specs=[SMEM, ANY, ANY, VMEM, ANY, VMEM],
         out_specs=VMEM,
         scratch_shapes=[
             pltpu.VMEM(activations.shape, BF16),
             pltpu.VMEM((depth, cols), BF16),
-            pltpu.VMEM(kv_rows.shape, BF16),
-            pltpu.SemaphoreType.DMA((q_chunks + 2,)),
+            pltpu.VMEM((rows, cols), F32),
+            pltpu.SemaphoreType.DMA((len(heights) + 1,)),
         ],
         compiler_params=pltpu.CompilerParams(vmem_limit_bytes=24 * MIB),
         cost_estimate=pl.CostEstimate(
-            flops=2 * rows * depth * cols, bytes_accessed=18 * MIB, transcendentals=0
+            flops=SPAN, bytes_accessed=18 * MIB, transcendentals=0
         ),
-    )(core, turns, in_hbm(activations), other, in_hbm(w_query), in_hbm(kv_rows))
+    )(core, turns, in_hbm(activations), other, in_hbm(w_query), in_vmem(kv_rows))
     parts = lax.all_to_all(partial, "wide", 0, 0, tiled=True)
     attended = pl.pallas_call(
         attend_kernel,
@@ -191,7 +213,7 @@
         out_specs=VMEM,
         compiler_params=pltpu.CompilerParams(vmem_limit_bytes=8 * MIB),
         cost_estimate=pl.CostEstimate(
-            flops=4 * heads * 2048 * HD, bytes_accessed=2 * MIB, transcendentals=heads * 2048
+            flops=SPAN, bytes_accessed=2 * MIB, transcendentals=heads * 2048
         ),
     )(lengths, turns, parts, cache_keys[0], cache_values[0])
     gathered = lax.all_to_all(attended, "wide", 0, 0, tiled=True)

time: 39 us -> 38.2 us (0.979)
  Pallas kernels: 10.7 us -> 9.91 us
    pallas_call x1 -> x2, Pallas kernels: 7.21 us -> 6.37 us  [the longest x1 6.29 us: local(): pl.pallas_call(functools.partial(project_kernel, heights), out_shape=pltp...]
  transfers between devices with their start and end apart: 2 -> 2, of which waited for: 1 -> 2; matrix products, arithmetic and copies ran while one was open for 0% -> 0% of each run, Pallas kernels for 0% -> 0%
where the time goes in v3:
time: 38.2 us; the launch traced here: 38 us
  blocking collectives  24.7 us (65%)
  Pallas kernels  9.91 us (26%)
  waiting for transfers between devices  1.3 us (3%)
  between operations  0.88 us (2%)
  other arithmetic  0.67 us (2%)
  starting transfers between devices  0.46 us (1%)
    all_to_all x1, blocking collectives, local(): parts = lax.all_to_all(partial, 'wide', 0, 0, tiled=True)  14.9 us
    all_to_all x1, blocking collectives, local(): gathered = lax.all_to_all(attended, 'wide', 0, 0, tiled=True)  9.77 us
    pallas_call x1, Pallas kernels, local(): pl.pallas_call(functools.partial(project_kernel, heights), out_shape=pltp...  6.29 us
    pallas_call x1, Pallas kernels, local(): pl.pallas_call(output_kernel, out_shape=[jax.ShapeDtypeStruct((rows // 2,...  2.39 us
    ppermute x1, waiting for transfers between devices, local(): return (keep + lax.ppermute(send, 'narrow', swap)).astype(BF16)  1.21 us
    pallas_call x1, Pallas kernels, local(): pl.pallas_call(attend_kernel, out_shape=jax.ShapeDtypeStruct((receivers,...  1.16 us
  transfers between devices with their start and end apart: 2, of which 2 were waited for; matrix products, arithmetic and copies ran while one was open for 0% of the time, Pallas kernels for 0%

profile of v3, /device:TPU:0, one launch (start us, length us, event | category | flops | bytes accessed | tf_op | source)
XLA Modules:
  0.0 38.0 jit_solution(18434585407606591845)
XLA Ops:
  0.0 0.0 copy-start
  0.0 0.5 %collective-permute-start = (bf16[4,2048]{1,0:T(4,128)(2,1)}, bf16[4,2048]{1,0:T(4,128)(2,1)S(1)}, u32[]{:S(2)}, u32[]{:S(2)}) collective-permute-start(bf16[4,2048]{1,0:T(4,128)(2,1)} %own_hbm.1), channel_id=1, source_target_pairs={{0,1},{1,0},{2,3},{3,2},{4,5},{5,4},{6,7},{7,6},{8,9},{9,8},{10,11... | collective-permute-start | bytes 49160 | tf_op jit(solution)/shard_map/ppermute | solution.py:189
  1.3 0.1 fusion
  1.3 0.1 shard_map.73.after_ref.turns_ref
  1.4 0.0 copy-start.1
  1.4 0.0 copy-start.2
  1.4 0.1 collective-permute-done.other_ref
  1.5 0.1 copy-done
  1.6 0.0 slice-start
  1.6 0.0 slice-start.1
  1.6 6.3 %shard_map.74 = f32[8,36,128]{2,1,0:T(8,128)S(1)} custom-call(s32[1]{0:T(128)} %bitcast.core_ref, f32[2,128]{1,0:T(2,128)S(1)} %shard_map.73.after_ref.turns_ref, bf16[4,2048]{1,0:T(4,128)(2,1)} %own_hbm.1, bf16[4,2048]{1,0:T(4,128)(2,1)S(1)} %collective-permute-done.other_ref, bf16[2048,4096]{1,0:T(8,128)(2,1)} %w_ref.2, bf16[8192,128]{1,0:T(8,128)(2,1)S(1)} %bitcast.9), custom_call_target="tpu_custom_call" | custom-call | flops 7000000000 | bytes 18874368 | tf_op jit(solution)/shard_map/pallas_call | solution.py:192
  7.9 0.0 slice-start.2
  7.9 14.9 %all_to_all.10.parts_ref = f32[8,36,128]{2,1,0:T(8,128)S(1)} all-to-all(f32[8,36,128]{2,1,0:T(8,128)S(1)} %shard_map.74), channel_id=1, replica_groups=mesh['grp'=2,'wide'=8,'narrow'=2] {'wide'}, dimensions={0} | all-to-all | bytes 294912 | tf_op jit(solution)/shard_map/all_to_all | solution.py:208
  22.8 0.0 copy-done.1
  22.8 0.0 copy-done.2
  22.8 0.0 slice-start.3
  22.8 1.2 %shard_map.75 = bf16[8,32,128]{2,1,0:T(8,128)(2,1)S(1)} custom-call(s32[1]{0:T(128)S(6)} %copy.8.length_ref, f32[2,128]{1,0:T(2,128)S(1)} %shard_map.73.after_ref.turns_ref, f32[8,36,128]{2,1,0:T(8,128)S(1)} %all_to_all.10.parts_ref, bf16[2,2048,128]{2,1,0:T(8,128)(2,1)S(1)} %bitcast.10, bf16[2,2048,128]{2,1,0:T(8,128)(2,1)S(1)} %bitcast.11), custom_call_target="tpu_custom_call" | custom-call | flops 7000000000 | bytes 2097152 | tf_op jit(solution)/shard_map/pallas_call | solution.py:209
  24.0 9.8 %all_to_all.11 = bf16[8,32,128]{2,1,0:T(8,128)(2,1)S(1)} all-to-all(bf16[8,32,128]{2,1,0:T(8,128)(2,1)S(1)} %shard_map.75), channel_id=1, replica_groups=mesh['grp'=2,'wide'=8,'narrow'=2] {'wide'}, dimensions={0} | all-to-all | bytes 131072 | tf_op jit(solution)/shard_map/all_to_all | solution.py:219
  33.8 0.0 slice-done
  33.8 0.0 slice-done.1
  33.8 0.0 slice-done.2
  33.8 0.0 slice-done.3
  33.8 2.4 %shard_map.76 = (f32[4,2048]{1,0:T(4,128)S(1)}, f32[4,2048]{1,0:T(4,128)S(1)}) custom-call(s32[1]{0:T(128)} %bitcast.core_ref, bf16[256,128]{1,0:T(8,128)(2,1)S(1)} %bitcast.8, bf16[4096,2048]{1,0:T(8,128)(2,1)S(1)} %bitcast.7), custom_call_target="tpu_custom_call" | custom-call | flops 134217728 | bytes 16777216 | tf_op jit(solution)/shard_map/pallas_call | solution.py:220
  36.2 0.0 collective-permute-start.1
  36.2 1.2 %collective-permute-done.1 = f32[4,2048]{1,0:T(4,128)S(1)} collective-permute-done((f32[4,2048]{1,0:T(4,128)S(1)}, f32[4,2048]{1,0:T(4,128)S(1)}, u32[]{:S(2)}, u32[]{:S(2)}) %collective-permute-start.1) | collective-permute-done | bytes 32800 | tf_op jit(solution)/shard_map/ppermute | solution.py:230
  37.4 0.6 %add_convert_fusion = bf16[4,2048]{1,0:T(4,128)(2,1)} fusion(f32[4,2048]{1,0:T(4,128)S(1)} %get-tuple-element.7, f32[4,2048]{1,0:T(4,128)S(1)} %collective-permute-done.1), kind=kLoop, calls=%fused_computation | loop fusion | flops 16384 | bytes 81920 | tf_op jit(solution)/shard_map/convert_element_type | solution.py:230
  (1 shorter events, 0.0 us)
Async XLA Ops:
  0.0 1.6 %copy-start = (bf16[2048,2,2,128]{3,2,1,0:T(2,128)(2,1)S(1)}, bf16[2048,2,2,128]{3,2,1,0:T(2,128)(2,1)}, u32[]{:S(2)}) copy-start(bf16[2048,2,2,128]{3,2,1,0:T(2,128)(2,1)} %param.9) | copy-start | bytes 6291460
  0.0 1.5 %collective-permute-start = (bf16[4,2048]{1,0:T(4,128)(2,1)}, bf16[4,2048]{1,0:T(4,128)(2,1)S(1)}, u32[]{:S(2)}, u32[]{:S(2)}) collective-permute-start(bf16[4,2048]{1,0:T(4,128)(2,1)} %own_hbm.1), channel_id=1, source_target_pairs={{0,1},{1,0},{2,3},{3,2},{4,5},{5,4},{6,7},{7,6},{8,9},{9,8},{10,11... | collective-permute-start | bytes 49160 | tf_op jit(solution)/shard_map/ppermute | solution.py:189
  1.4 21.4 %copy-start.1 = (bf16[1,2,2048,128]{3,2,1,0:T(8,128)(2,1)S(1)}, bf16[1,2,2048,128]{3,2,1,0:T(8,128)(2,1)}, u32[]{:S(2)}) copy-start(bf16[1,2,2048,128]{3,2,1,0:T(8,128)(2,1)} %param.10) | copy-start | bytes 3145732
  1.4 21.4 %copy-start.2 = (bf16[1,2,2048,128]{3,2,1,0:T(8,128)(2,1)S(1)}, bf16[1,2,2048,128]{3,2,1,0:T(8,128)(2,1)}, u32[]{:S(2)}) copy-start(bf16[1,2,2048,128]{3,2,1,0:T(8,128)(2,1)} %param.11) | copy-start | bytes 3145732
  1.6 32.2 %slice-start = ((s8[16777216]{0:T(1024)(128)(4,1)}), s8[4194304]{0:T(1024)(128)(4,1)S(1)}, s32[]{:S(2)}) async-start(s8[16777216]{0:T(1024)(128)(4,1)} %bitcast.6), calls=%async_computation.2 | async-start | bytes 8388608
  1.6 32.2 %slice-start.1 = ((s8[16777216]{0:T(1024)(128)(4,1)}), s8[4194304]{0:T(1024)(128)(4,1)S(1)}, s32[]{:S(2)}) async-start(s8[16777216]{0:T(1024)(128)(4,1)} %bitcast.6), calls=%async_computation.3 | async-start | bytes 8388608
  7.9 25.9 %slice-start.2 = ((s8[16777216]{0:T(1024)(128)(4,1)}), s8[4194304]{0:T(1024)(128)(4,1)S(1)}, s32[]{:S(2)}) async-start(s8[16777216]{0:T(1024)(128)(4,1)} %bitcast.6), calls=%async_computation.4 | async-start | bytes 8388608
  22.8 10.9 %slice-start.3 = ((s8[16777216]{0:T(1024)(128)(4,1)}), s8[4194304]{0:T(1024)(128)(4,1)S(1)}, s32[]{:S(2)}) async-start(s8[16777216]{0:T(1024)(128)(4,1)} %bitcast.6), calls=%async_computation.5 | async-start | bytes 8388608
  36.2 1.2 %collective-permute-start.1 = (f32[4,2048]{1,0:T(4,128)S(1)}, f32[4,2048]{1,0:T(4,128)S(1)}, u32[]{:S(2)}, u32[]{:S(2)}) collective-permute-start(f32[4,2048]{1,0:T(4,128)S(1)} %get-tuple-element.8), channel_id=1, source_target_pairs={{0,1},{1,0},{2,3},{3,2},{4,5},{5,4},{6,7},{7,6},{8,9},{9,8},{10,11... | collective-permute-start | bytes 98312 | tf_op jit(solution)/shard_map/ppermute | solution.py:230

commit v4 on v3

--- a/solution.py
+++ b/solution.py
@@ -105,30 +105,35 @@
     rotated = rotated.astype(BF16)
     scale = 1.0 / math.sqrt(HD)
     length = length_ref[0]
-    visible = lax.broadcasted_iota(jnp.int32, (group, slots), 1) < length
-    attended = []
+    visible = lax.broadcasted_iota(jnp.int32, (heads, slots), 1) < length
+    groups = [slice(k * group, (k + 1) * group) for k in range(kv_heads)]
+    scores = [
+        lax.dot_general(
+            rotated[rows], keys_ref[k], (((1,), (1,)), ((), ())), preferred_element_type=F32
+        )
+        for k, rows in enumerate(groups)
+    ]
+    scores = jnp.concatenate(scores, axis=0) * scale
+    new_key, new_value = [], []
     for k in range(kv_heads):
-        query = rotated[k * group : (k + 1) * group]
-        new_key = rotated[heads + 2 * k : heads + 2 * k + 1].astype(F32)
-        new_value = summed[heads + 2 * k + 1 : heads + 2 * k + 2].astype(BF16).astype(F32)
-        scores = (
-            lax.dot_general(
-                query, keys_ref[k], (((1,), (1,)), ((), ())), preferred_element_type=F32
-            )
-            * scale
-        )
-        own = jnp.sum(query.astype(F32) * new_key, axis=-1, keepdims=True) * scale
-        scores = jnp.where(visible, scores, -1e30)
-        top = jnp.maximum(jnp.max(scores, axis=-1, keepdims=True), own)
-        weights = jnp.where(visible, jnp.exp(scores - top), 0.0)
-        own_weight = jnp.exp(own - top)
-        denominator = jnp.sum(weights, axis=-1, keepdims=True) + own_weight
-        inverse = 1.0 / denominator
-        probabilities = (weights * inverse).astype(BF16)
-        own_prob = (own_weight * inverse).astype(BF16).astype(F32)
-        result = jnp.dot(probabilities, values_ref[k], preferred_element_type=F32)
-        attended.append((result + own_prob * new_value).astype(BF16))
-    block = jnp.concatenate(attended, axis=0)
+        at = heads + 2 * k
+        new_key.append(jnp.broadcast_to(rotated[at : at + 1].astype(F32), (group, HD)))
+        value = summed[at + 1 : at + 2].astype(BF16).astype(F32)
+        new_value.append(jnp.broadcast_to(value, (group, HD)))
+    new_key, new_value = jnp.concatenate(new_key, axis=0), jnp.concatenate(new_value, axis=0)
+    own = jnp.sum(rotated[:heads].astype(F32) * new_key, axis=-1, keepdims=True) * scale
+    scores = jnp.where(visible, scores, -1e30)
+    top = jnp.maximum(jnp.max(scores, axis=-1, keepdims=True), own)
+    weights = jnp.where(visible, jnp.exp(scores - top), 0.0)
+    own_weight = jnp.exp(own - top)
+    inverse = 1.0 / (jnp.sum(weights, axis=-1, keepdims=True) + own_weight)
+    probabilities = (weights * inverse).astype(BF16)
+    own_prob = (own_weight * inverse).astype(BF16).astype(F32)
+    result = [
+        jnp.dot(probabilities[rows], values_ref[k], preferred_element_type=F32)
+        for k, rows in enumerate(groups)
+    ]
+    block = (jnp.concatenate(result, axis=0) + own_prob * new_value).astype(BF16)
     for i in range(out_ref.shape[0]):
         out_ref[i] = block
 

time: 38.2 us -> 37.9 us (level)
  no operation moved by 1% of the time
where the time goes in v4:
time: 37.9 us; the launch traced here: 37.6 us
  blocking collectives  24.7 us (65%)
  Pallas kernels  9.55 us (25%)
  waiting for transfers between devices  1.3 us (3%)
  between operations  0.88 us (2%)
  other arithmetic  0.67 us (2%)
  starting transfers between devices  0.46 us (1%)
    all_to_all x1, blocking collectives, local(): parts = lax.all_to_all(partial, 'wide', 0, 0, tiled=True)  14.9 us
    all_to_all x1, blocking collectives, local(): gathered = lax.all_to_all(attended, 'wide', 0, 0, tiled=True)  9.77 us
    pallas_call x1, Pallas kernels, local(): pl.pallas_call(functools.partial(project_kernel, heights), out_shape=pltp...  6.29 us
    pallas_call x1, Pallas kernels, local(): pl.pallas_call(output_kernel, out_shape=[jax.ShapeDtypeStruct((rows // 2,...  2.39 us
    ppermute x1, waiting for transfers between devices, local(): return (keep + lax.ppermute(send, 'narrow', swap)).astype(BF16)  1.21 us
    pallas_call x1, Pallas kernels, local(): pl.pallas_call(attend_kernel, out_shape=jax.ShapeDtypeStruct((receivers,...  0.8 us
  transfers between devices with their start and end apart: 2, of which 2 were waited for; matrix products, arithmetic and copies ran while one was open for 0% of the time, Pallas kernels for 0%

profile of v4, /device:TPU:0, one launch (start us, length us, event | category | flops | bytes accessed | tf_op | source)
XLA Modules:
  0.0 37.6 jit_solution(2805462272476578822)
XLA Ops:
  0.0 0.0 copy-start
  0.0 0.5 %collective-permute-start = (bf16[4,2048]{1,0:T(4,128)(2,1)}, bf16[4,2048]{1,0:T(4,128)(2,1)S(1)}, u32[]{:S(2)}, u32[]{:S(2)}) collective-permute-start(bf16[4,2048]{1,0:T(4,128)(2,1)} %own_hbm.1), channel_id=1, source_target_pairs={{0,1},{1,0},{2,3},{3,2},{4,5},{5,4},{6,7},{7,6},{8,9},{9,8},{10,11... | collective-permute-start | bytes 49160 | tf_op jit(solution)/shard_map/ppermute | solution.py:194
  1.3 0.1 fusion
  1.3 0.1 shard_map.73.after_ref.turns_ref
  1.4 0.0 copy-start.1
  1.4 0.0 copy-start.2
  1.4 0.1 collective-permute-done.other_ref
  1.5 0.1 copy-done
  1.6 0.0 slice-start
  1.6 0.0 slice-start.1
  1.6 6.3 %shard_map.74 = f32[8,36,128]{2,1,0:T(8,128)S(1)} custom-call(s32[1]{0:T(128)} %bitcast.core_ref, f32[2,128]{1,0:T(2,128)S(1)} %shard_map.73.after_ref.turns_ref, bf16[4,2048]{1,0:T(4,128)(2,1)} %own_hbm.1, bf16[4,2048]{1,0:T(4,128)(2,1)S(1)} %collective-permute-done.other_ref, bf16[2048,4096]{1,0:T(8,128)(2,1)} %w_ref.2, bf16[8192,128]{1,0:T(8,128)(2,1)S(1)} %bitcast.9), custom_call_target="tpu_custom_call" | custom-call | flops 7000000000 | bytes 18874368 | tf_op jit(solution)/shard_map/pallas_call | solution.py:197
  7.9 0.0 slice-start.2
  7.9 14.9 %all_to_all.10.parts_ref = f32[8,36,128]{2,1,0:T(8,128)S(1)} all-to-all(f32[8,36,128]{2,1,0:T(8,128)S(1)} %shard_map.74), channel_id=1, replica_groups=mesh['grp'=2,'wide'=8,'narrow'=2] {'wide'}, dimensions={0} | all-to-all | bytes 294912 | tf_op jit(solution)/shard_map/all_to_all | solution.py:213
  22.8 0.0 copy-done.1
  22.8 0.0 copy-done.2
  22.8 0.0 slice-start.3
  22.8 0.8 %shard_map.75 = bf16[8,32,128]{2,1,0:T(8,128)(2,1)S(1)} custom-call(s32[1]{0:T(128)S(6)} %copy.8.length_ref, f32[2,128]{1,0:T(2,128)S(1)} %shard_map.73.after_ref.turns_ref, f32[8,36,128]{2,1,0:T(8,128)S(1)} %all_to_all.10.parts_ref, bf16[2,2048,128]{2,1,0:T(8,128)(2,1)S(1)} %bitcast.10, bf16[2,2048,128]{2,1,0:T(8,128)(2,1)S(1)} %bitcast.11), custom_call_target="tpu_custom_call" | custom-call | flops 7000000000 | bytes 2097152 | tf_op jit(solution)/shard_map/pallas_call | solution.py:214
  23.6 9.8 %all_to_all.11 = bf16[8,32,128]{2,1,0:T(8,128)(2,1)S(1)} all-to-all(bf16[8,32,128]{2,1,0:T(8,128)(2,1)S(1)} %shard_map.75), channel_id=1, replica_groups=mesh['grp'=2,'wide'=8,'narrow'=2] {'wide'}, dimensions={0} | all-to-all | bytes 131072 | tf_op jit(solution)/shard_map/all_to_all | solution.py:224
  33.4 0.0 slice-done
  33.4 0.0 slice-done.1
  33.4 0.0 slice-done.2
  33.4 0.0 slice-done.3
  33.4 2.4 %shard_map.76 = (f32[4,2048]{1,0:T(4,128)S(1)}, f32[4,2048]{1,0:T(4,128)S(1)}) custom-call(s32[1]{0:T(128)} %bitcast.core_ref, bf16[256,128]{1,0:T(8,128)(2,1)S(1)} %bitcast.8, bf16[4096,2048]{1,0:T(8,128)(2,1)S(1)} %bitcast.7), custom_call_target="tpu_custom_call" | custom-call | flops 134217728 | bytes 16777216 | tf_op jit(solution)/shard_map/pallas_call | solution.py:225
  35.8 0.0 collective-permute-start.1
  35.8 1.2 %collective-permute-done.1 = f32[4,2048]{1,0:T(4,128)S(1)} collective-permute-done((f32[4,2048]{1,0:T(4,128)S(1)}, f32[4,2048]{1,0:T(4,128)S(1)}, u32[]{:S(2)}, u32[]{:S(2)}) %collective-permute-start.1) | collective-permute-done | bytes 32800 | tf_op jit(solution)/shard_map/ppermute | solution.py:235
  37.0 0.6 %add_convert_fusion = bf16[4,2048]{1,0:T(4,128)(2,1)} fusion(f32[4,2048]{1,0:T(4,128)S(1)} %get-tuple-element.7, f32[4,2048]{1,0:T(4,128)S(1)} %collective-permute-done.1), kind=kLoop, calls=%fused_computation | loop fusion | flops 16384 | bytes 81920 | tf_op jit(solution)/shard_map/convert_element_type | solution.py:235
  (1 shorter events, 0.0 us)
Async XLA Ops:
  0.0 1.6 %copy-start = (bf16[2048,2,2,128]{3,2,1,0:T(2,128)(2,1)S(1)}, bf16[2048,2,2,128]{3,2,1,0:T(2,128)(2,1)}, u32[]{:S(2)}) copy-start(bf16[2048,2,2,128]{3,2,1,0:T(2,128)(2,1)} %param.9) | copy-start | bytes 6291460
  0.0 1.5 %collective-permute-start = (bf16[4,2048]{1,0:T(4,128)(2,1)}, bf16[4,2048]{1,0:T(4,128)(2,1)S(1)}, u32[]{:S(2)}, u32[]{:S(2)}) collective-permute-start(bf16[4,2048]{1,0:T(4,128)(2,1)} %own_hbm.1), channel_id=1, source_target_pairs={{0,1},{1,0},{2,3},{3,2},{4,5},{5,4},{6,7},{7,6},{8,9},{9,8},{10,11... | collective-permute-start | bytes 49160 | tf_op jit(solution)/shard_map/ppermute | solution.py:194
  1.4 21.4 %copy-start.1 = (bf16[1,2,2048,128]{3,2,1,0:T(8,128)(2,1)S(1)}, bf16[1,2,2048,128]{3,2,1,0:T(8,128)(2,1)}, u32[]{:S(2)}) copy-start(bf16[1,2,2048,128]{3,2,1,0:T(8,128)(2,1)} %param.10) | copy-start | bytes 3145732
  1.4 21.4 %copy-start.2 = (bf16[1,2,2048,128]{3,2,1,0:T(8,128)(2,1)S(1)}, bf16[1,2,2048,128]{3,2,1,0:T(8,128)(2,1)}, u32[]{:S(2)}) copy-start(bf16[1,2,2048,128]{3,2,1,0:T(8,128)(2,1)} %param.11) | copy-start | bytes 3145732
  1.6 31.8 %slice-start = ((s8[16777216]{0:T(1024)(128)(4,1)}), s8[4194304]{0:T(1024)(128)(4,1)S(1)}, s32[]{:S(2)}) async-start(s8[16777216]{0:T(1024)(128)(4,1)} %bitcast.6), calls=%async_computation.2 | async-start | bytes 8388608
  1.6 31.8 %slice-start.1 = ((s8[16777216]{0:T(1024)(128)(4,1)}), s8[4194304]{0:T(1024)(128)(4,1)S(1)}, s32[]{:S(2)}) async-start(s8[16777216]{0:T(1024)(128)(4,1)} %bitcast.6), calls=%async_computation.3 | async-start | bytes 8388608
  7.9 25.5 %slice-start.2 = ((s8[16777216]{0:T(1024)(128)(4,1)}), s8[4194304]{0:T(1024)(128)(4,1)S(1)}, s32[]{:S(2)}) async-start(s8[16777216]{0:T(1024)(128)(4,1)} %bitcast.6), calls=%async_computation.4 | async-start | bytes 8388608
  22.8 10.6 %slice-start.3 = ((s8[16777216]{0:T(1024)(128)(4,1)}), s8[4194304]{0:T(1024)(128)(4,1)S(1)}, s32[]{:S(2)}) async-start(s8[16777216]{0:T(1024)(128)(4,1)} %bitcast.6), calls=%async_computation.5 | async-start | bytes 8388608
  35.8 1.2 %collective-permute-start.1 = (f32[4,2048]{1,0:T(4,128)S(1)}, f32[4,2048]{1,0:T(4,128)S(1)}, u32[]{:S(2)}, u32[]{:S(2)}) collective-permute-start(f32[4,2048]{1,0:T(4,128)S(1)} %get-tuple-element.8), channel_id=1, source_target_pairs={{0,1},{1,0},{2,3},{3,2},{4,5},{5,4},{6,7},{7,6},{8,9},{9,8},{10,11... | collective-permute-start | bytes 98312 | tf_op jit(solution)/shard_map/ppermute | solution.py:235

commit v5 on v4

--- a/solution.py
+++ b/solution.py
@@ -9,6 +9,7 @@
 from jax.sharding import PartitionSpec as P
 
 HD = 128
+SUB = 4
 ROPE_BASE = 500000.0
 MIB = 2**20
 F32, BF16 = jnp.float32, jnp.bfloat16
@@ -78,7 +79,7 @@
         )
         total = part if total is None else total + part
     for p in range(parts):
-        sums[:, heads + p, :] = total[p * count : (p + 1) * count]
+        sums[:, (heads + p) // SUB, (heads + p) % SUB, :] = total[p * count : (p + 1) * count]
 
     for c, (at, height) in enumerate(spans):
         copies[c].wait()
@@ -90,15 +91,16 @@
         if c < len(spans) - 1:
             held[...] = block
     for h in range(heads):
-        sums[:, h, :] = block[:, h * HD : (h + 1) * HD]
+        sums[:, h // SUB, h % SUB, :] = block[:, h * HD : (h + 1) * HD]
 
 
 def attend_kernel(length_ref, turns_ref, parts_ref, keys_ref, values_ref, out_ref):
     summed = parts_ref[0]
     for i in range(1, parts_ref.shape[0]):
         summed = summed + parts_ref[i]
+    summed = jnp.concatenate([summed[i] for i in range(summed.shape[0])], axis=0)
     kv_heads = keys_ref.shape[0]
-    heads = parts_ref.shape[1] - 2 * kv_heads
+    heads = summed.shape[0] - 2 * kv_heads
     group = heads // kv_heads
     slots = keys_ref.shape[1]
     rotated = summed * turns_ref[:1] + pltpu.roll(summed, HD // 2, 1) * turns_ref[1:]
@@ -192,11 +194,11 @@
     )(cosine, sine)
 
     other = lax.ppermute(activations, "narrow", swap)
-    heights = [depth // 8] * 7 + [depth // 16] * 2 if depth % 256 == 0 else [depth]
+    heights = [depth // 8] * 7 + [depth // 16] + [depth // 32] * 2 if depth % 512 == 0 else [depth]
     kv_rows = w_keyval.reshape(depth * kv_heads * 2, HD)
     partial = pl.pallas_call(
         functools.partial(project_kernel, heights),
-        out_shape=pltpu.VMEM((rows, heads + 2 * kv_heads, HD), F32),
+        out_shape=pltpu.VMEM((rows, (heads + 2 * kv_heads) // SUB, SUB, HD), F32),
         in_specs=[SMEM, ANY, ANY, VMEM, ANY, VMEM],
         out_specs=VMEM,
         scratch_shapes=[

time: 37.9 us -> 37.5 us (0.989)
  blocking collectives: 24.7 us -> 24.3 us
where the time goes in v5:
time: 37.5 us; the launch traced here: 37.3 us
  blocking collectives  24.3 us (65%)
  Pallas kernels  9.53 us (25%)
  waiting for transfers between devices  1.3 us (3%)
  between operations  0.88 us (2%)
  other arithmetic  0.67 us (2%)
  starting transfers between devices  0.46 us (1%)
    all_to_all x1, blocking collectives, local(): parts = lax.all_to_all(partial, 'wide', 0, 0, tiled=True)  14.8 us
    all_to_all x1, blocking collectives, local(): gathered = lax.all_to_all(attended, 'wide', 0, 0, tiled=True)  9.55 us
    pallas_call x1, Pallas kernels, local(): pl.pallas_call(functools.partial(project_kernel, heights), out_shape=pltp...  6.27 us
    pallas_call x1, Pallas kernels, local(): pl.pallas_call(output_kernel, out_shape=[jax.ShapeDtypeStruct((rows // 2,...  2.39 us
    ppermute x1, waiting for transfers between devices, local(): return (keep + lax.ppermute(send, 'narrow', swap)).astype(BF16)  1.21 us
    pallas_call x1, Pallas kernels, local(): pl.pallas_call(attend_kernel, out_shape=jax.ShapeDtypeStruct((receivers,...  0.8 us
  transfers between devices with their start and end apart: 2, of which 2 were waited for; matrix products, arithmetic and copies ran while one was open for 0% of the time, Pallas kernels for 0%

profile of v5, /device:TPU:0, one launch (start us, length us, event | category | flops | bytes accessed | tf_op | source)
XLA Modules:
  0.0 37.3 jit_solution(10101591679607200110)
XLA Ops:
  0.0 0.0 copy-start
  0.0 0.5 %collective-permute-start = (bf16[4,2048]{1,0:T(4,128)(2,1)}, bf16[4,2048]{1,0:T(4,128)(2,1)S(1)}, u32[]{:S(2)}, u32[]{:S(2)}) collective-permute-start(bf16[4,2048]{1,0:T(4,128)(2,1)} %own_hbm.1), channel_id=1, source_target_pairs={{0,1},{1,0},{2,3},{3,2},{4,5},{5,4},{6,7},{7,6},{8,9},{9,8},{10,11... | collective-permute-start | bytes 49160 | tf_op jit(solution)/shard_map/ppermute | solution.py:196
  1.3 0.1 fusion
  1.3 0.1 shard_map.73.after_ref.turns_ref
  1.4 0.0 copy-start.1
  1.4 0.0 copy-start.2
  1.4 0.1 collective-permute-done.other_ref
  1.5 0.1 copy-done
  1.6 0.0 slice-start
  1.6 0.0 slice-start.1
  1.6 6.3 %shard_map.74 = f32[8,9,4,128]{3,2,1,0:T(4,128)S(1)} custom-call(s32[1]{0:T(128)} %bitcast.core_ref, f32[2,128]{1,0:T(2,128)S(1)} %shard_map.73.after_ref.turns_ref, bf16[4,2048]{1,0:T(4,128)(2,1)} %own_hbm.1, bf16[4,2048]{1,0:T(4,128)(2,1)S(1)} %collective-permute-done.other_ref, bf16[2048,4096]{1,0:T(8,128)(2,1)} %w_ref.2, bf16[8192,128]{1,0:T(8,128)(2,1)S(1)} %bitcast.9), custom_call_target="tpu_custom_call" | custom-call | flops 7000000000 | bytes 18874368 | tf_op jit(solution)/shard_map/pallas_call | solution.py:199
  7.9 0.0 slice-start.2
  7.9 14.8 %all_to_all.10.parts_ref = f32[8,9,4,128]{3,2,1,0:T(4,128)S(1)} all-to-all(f32[8,9,4,128]{3,2,1,0:T(4,128)S(1)} %shard_map.74), channel_id=1, replica_groups=mesh['grp'=2,'wide'=8,'narrow'=2] {'wide'}, dimensions={0} | all-to-all | bytes 294912 | tf_op jit(solution)/shard_map/all_to_all | solution.py:215
  22.7 0.0 copy-done.1
  22.7 0.0 copy-done.2
  22.7 0.0 slice-start.3
  22.7 0.8 %shard_map.75 = bf16[8,32,128]{2,1,0:T(8,128)(2,1)S(1)} custom-call(s32[1]{0:T(128)S(6)} %copy.8.length_ref, f32[2,128]{1,0:T(2,128)S(1)} %shard_map.73.after_ref.turns_ref, f32[8,9,4,128]{3,2,1,0:T(4,128)S(1)} %all_to_all.10.parts_ref, bf16[2,2048,128]{2,1,0:T(8,128)(2,1)S(1)} %bitcast.10, bf16[2,2048,128]{2,1,0:T(8,128)(2,1)S(1)} %bitcast.11), custom_call_target="tpu_custom_call" | custom-call | flops 7000000000 | bytes 2097152 | tf_op jit(solution)/shard_map/pallas_call | solution.py:216
  23.5 9.5 %all_to_all.11 = bf16[8,32,128]{2,1,0:T(8,128)(2,1)S(1)} all-to-all(bf16[8,32,128]{2,1,0:T(8,128)(2,1)S(1)} %shard_map.75), channel_id=1, replica_groups=mesh['grp'=2,'wide'=8,'narrow'=2] {'wide'}, dimensions={0} | all-to-all | bytes 131072 | tf_op jit(solution)/shard_map/all_to_all | solution.py:226
  33.0 0.0 slice-done
  33.0 0.0 slice-done.1
  33.0 0.0 slice-done.2
  33.0 0.0 slice-done.3
  33.1 2.4 %shard_map.76 = (f32[4,2048]{1,0:T(4,128)S(1)}, f32[4,2048]{1,0:T(4,128)S(1)}) custom-call(s32[1]{0:T(128)} %bitcast.core_ref, bf16[256,128]{1,0:T(8,128)(2,1)S(1)} %bitcast.8, bf16[4096,2048]{1,0:T(8,128)(2,1)S(1)} %bitcast.7), custom_call_target="tpu_custom_call" | custom-call | flops 134217728 | bytes 16777216 | tf_op jit(solution)/shard_map/pallas_call | solution.py:227
  35.4 0.0 collective-permute-start.1
  35.4 1.2 %collective-permute-done.1 = f32[4,2048]{1,0:T(4,128)S(1)} collective-permute-done((f32[4,2048]{1,0:T(4,128)S(1)}, f32[4,2048]{1,0:T(4,128)S(1)}, u32[]{:S(2)}, u32[]{:S(2)}) %collective-permute-start.1) | collective-permute-done | bytes 32800 | tf_op jit(solution)/shard_map/ppermute | solution.py:237
  36.7 0.6 %add_convert_fusion = bf16[4,2048]{1,0:T(4,128)(2,1)} fusion(f32[4,2048]{1,0:T(4,128)S(1)} %get-tuple-element.7, f32[4,2048]{1,0:T(4,128)S(1)} %collective-permute-done.1), kind=kLoop, calls=%fused_computation | loop fusion | flops 16384 | bytes 81920 | tf_op jit(solution)/shard_map/convert_element_type | solution.py:237
  (1 shorter events, 0.0 us)
Async XLA Ops:
  0.0 1.6 %copy-start = (bf16[2048,2,2,128]{3,2,1,0:T(2,128)(2,1)S(1)}, bf16[2048,2,2,128]{3,2,1,0:T(2,128)(2,1)}, u32[]{:S(2)}) copy-start(bf16[2048,2,2,128]{3,2,1,0:T(2,128)(2,1)} %param.9) | copy-start | bytes 6291460
  0.0 1.5 %collective-permute-start = (bf16[4,2048]{1,0:T(4,128)(2,1)}, bf16[4,2048]{1,0:T(4,128)(2,1)S(1)}, u32[]{:S(2)}, u32[]{:S(2)}) collective-permute-start(bf16[4,2048]{1,0:T(4,128)(2,1)} %own_hbm.1), channel_id=1, source_target_pairs={{0,1},{1,0},{2,3},{3,2},{4,5},{5,4},{6,7},{7,6},{8,9},{9,8},{10,11... | collective-permute-start | bytes 49160 | tf_op jit(solution)/shard_map/ppermute | solution.py:196
  1.4 21.3 %copy-start.1 = (bf16[1,2,2048,128]{3,2,1,0:T(8,128)(2,1)S(1)}, bf16[1,2,2048,128]{3,2,1,0:T(8,128)(2,1)}, u32[]{:S(2)}) copy-start(bf16[1,2,2048,128]{3,2,1,0:T(8,128)(2,1)} %param.10) | copy-start | bytes 3145732
  1.4 21.3 %copy-start.2 = (bf16[1,2,2048,128]{3,2,1,0:T(8,128)(2,1)S(1)}, bf16[1,2,2048,128]{3,2,1,0:T(8,128)(2,1)}, u32[]{:S(2)}) copy-start(bf16[1,2,2048,128]{3,2,1,0:T(8,128)(2,1)} %param.11) | copy-start | bytes 3145732
  1.6 31.4 %slice-start = ((s8[16777216]{0:T(1024)(128)(4,1)}), s8[4194304]{0:T(1024)(128)(4,1)S(1)}, s32[]{:S(2)}) async-start(s8[16777216]{0:T(1024)(128)(4,1)} %bitcast.6), calls=%async_computation.2 | async-start | bytes 8388608
  1.6 31.4 %slice-start.1 = ((s8[16777216]{0:T(1024)(128)(4,1)}), s8[4194304]{0:T(1024)(128)(4,1)S(1)}, s32[]{:S(2)}) async-start(s8[16777216]{0:T(1024)(128)(4,1)} %bitcast.6), calls=%async_computation.3 | async-start | bytes 8388608
  7.9 25.2 %slice-start.2 = ((s8[16777216]{0:T(1024)(128)(4,1)}), s8[4194304]{0:T(1024)(128)(4,1)S(1)}, s32[]{:S(2)}) async-start(s8[16777216]{0:T(1024)(128)(4,1)} %bitcast.6), calls=%async_computation.4 | async-start | bytes 8388608
  22.7 10.4 %slice-start.3 = ((s8[16777216]{0:T(1024)(128)(4,1)}), s8[4194304]{0:T(1024)(128)(4,1)S(1)}, s32[]{:S(2)}) async-start(s8[16777216]{0:T(1024)(128)(4,1)} %bitcast.6), calls=%async_computation.5 | async-start | bytes 8388608
  35.4 1.2 %collective-permute-start.1 = (f32[4,2048]{1,0:T(4,128)S(1)}, f32[4,2048]{1,0:T(4,128)S(1)}, u32[]{:S(2)}, u32[]{:S(2)}) collective-permute-start(f32[4,2048]{1,0:T(4,128)S(1)} %get-tuple-element.8), channel_id=1, source_target_pairs={{0,1},{1,0},{2,3},{3,2},{4,5},{5,4},{6,7},{7,6},{8,9},{9,8},{10,11... | collective-permute-start | bytes 98312 | tf_op jit(solution)/shard_map/ppermute | solution.py:237

commit v6 on v5

--- a/solution.py
+++ b/solution.py
@@ -68,19 +68,6 @@
     spread = jnp.where(spread_to // parts == spread_of, 1.0, 0.0).astype(BF16)
     repeated = jnp.dot(stacked, spread, preferred_element_type=F32)
     slot = lax.broadcasted_iota(jnp.int32, (count, parts * HD), 1) % parts
-    total = None
-    for t in range(tiles):
-        block = repeated[t * count : (t + 1) * count]
-        left = jnp.concatenate(
-            [jnp.where(slot == p, block, 0.0) for p in range(parts)], axis=0
-        ).astype(BF16)
-        part = jnp.dot(
-            left, kv_ref[t * parts * HD : (t + 1) * parts * HD, :], preferred_element_type=F32
-        )
-        total = part if total is None else total + part
-    for p in range(parts):
-        sums[:, (heads + p) // SUB, (heads + p) % SUB, :] = total[p * count : (p + 1) * count]
-
     for c, (at, height) in enumerate(spans):
         copies[c].wait()
         block = jnp.dot(
@@ -90,6 +77,19 @@
             block = block + held[...]
         if c < len(spans) - 1:
             held[...] = block
+        if c == min(1, len(spans) - 1):
+            total = None
+            for t in range(tiles):
+                piece = repeated[t * count : (t + 1) * count]
+                left = jnp.concatenate(
+                    [jnp.where(slot == p, piece, 0.0) for p in range(parts)], axis=0
+                ).astype(BF16)
+                part = jnp.dot(
+                    left, kv_ref[t * parts * HD : (t + 1) * parts * HD, :], preferred_element_type=F32
+                )
+                total = part if total is None else total + part
+            for p in range(parts):
+                sums[:, (heads + p) // SUB, (heads + p) % SUB, :] = total[p * count : (p + 1) * count]
     for h in range(heads):
         sums[:, h // SUB, h % SUB, :] = block[:, h * HD : (h + 1) * HD]
 

time: 37.5 us -> 37.5 us (level)
  no operation moved by 1% of the time
where the time goes in v6:
time: 37.5 us; the launch traced here: 37.3 us
  blocking collectives  24.3 us (65%)
  Pallas kernels  9.53 us (25%)
  waiting for transfers between devices  1.3 us (3%)
  between operations  0.88 us (2%)
  other arithmetic  0.67 us (2%)
  starting transfers between devices  0.46 us (1%)
    all_to_all x1, blocking collectives, local(): parts = lax.all_to_all(partial, 'wide', 0, 0, tiled=True)  14.8 us
    all_to_all x1, blocking collectives, local(): gathered = lax.all_to_all(attended, 'wide', 0, 0, tiled=True)  9.55 us
    pallas_call x1, Pallas kernels, local(): pl.pallas_call(functools.partial(project_kernel, heights), out_shape=pltp...  6.27 us
    pallas_call x1, Pallas kernels, local(): pl.pallas_call(output_kernel, out_shape=[jax.ShapeDtypeStruct((rows // 2,...  2.39 us
    ppermute x1, waiting for transfers between devices, local(): return (keep + lax.ppermute(send, 'narrow', swap)).astype(BF16)  1.21 us
    pallas_call x1, Pallas kernels, local(): pl.pallas_call(attend_kernel, out_shape=jax.ShapeDtypeStruct((receivers,...  0.8 us
  transfers between devices with their start and end apart: 2, of which 2 were waited for; matrix products, arithmetic and copies ran while one was open for 0% of the time, Pallas kernels for 0%

profile of v6, /device:TPU:0, one launch (start us, length us, event | category | flops | bytes accessed | tf_op | source)
XLA Modules:
  0.0 37.3 jit_solution(4709567481807669111)
XLA Ops:
  0.0 0.0 copy-start
  0.0 0.5 %collective-permute-start = (bf16[4,2048]{1,0:T(4,128)(2,1)}, bf16[4,2048]{1,0:T(4,128)(2,1)S(1)}, u32[]{:S(2)}, u32[]{:S(2)}) collective-permute-start(bf16[4,2048]{1,0:T(4,128)(2,1)} %own_hbm.1), channel_id=1, source_target_pairs={{0,1},{1,0},{2,3},{3,2},{4,5},{5,4},{6,7},{7,6},{8,9},{9,8},{10,11... | collective-permute-start | bytes 49160 | tf_op jit(solution)/shard_map/ppermute | solution.py:196
  1.3 0.1 fusion
  1.3 0.1 shard_map.73.after_ref.turns_ref
  1.4 0.0 copy-start.1
  1.4 0.0 copy-start.2
  1.4 0.1 collective-permute-done.other_ref
  1.5 0.1 copy-done
  1.6 0.0 slice-start
  1.6 0.0 slice-start.1
  1.6 6.3 %shard_map.74 = f32[8,9,4,128]{3,2,1,0:T(4,128)S(1)} custom-call(s32[1]{0:T(128)} %bitcast.core_ref, f32[2,128]{1,0:T(2,128)S(1)} %shard_map.73.after_ref.turns_ref, bf16[4,2048]{1,0:T(4,128)(2,1)} %own_hbm.1, bf16[4,2048]{1,0:T(4,128)(2,1)S(1)} %collective-permute-done.other_ref, bf16[2048,4096]{1,0:T(8,128)(2,1)} %w_ref.2, bf16[8192,128]{1,0:T(8,128)(2,1)S(1)} %bitcast.9), custom_call_target="tpu_custom_call" | custom-call | flops 7000000000 | bytes 18874368 | tf_op jit(solution)/shard_map/pallas_call | solution.py:199
  7.9 0.0 slice-start.2
  7.9 14.8 %all_to_all.10.parts_ref = f32[8,9,4,128]{3,2,1,0:T(4,128)S(1)} all-to-all(f32[8,9,4,128]{3,2,1,0:T(4,128)S(1)} %shard_map.74), channel_id=1, replica_groups=mesh['grp'=2,'wide'=8,'narrow'=2] {'wide'}, dimensions={0} | all-to-all | bytes 294912 | tf_op jit(solution)/shard_map/all_to_all | solution.py:215
  22.7 0.0 copy-done.1
  22.7 0.0 copy-done.2
  22.7 0.0 slice-start.3
  22.7 0.8 %shard_map.75 = bf16[8,32,128]{2,1,0:T(8,128)(2,1)S(1)} custom-call(s32[1]{0:T(128)S(6)} %copy.8.length_ref, f32[2,128]{1,0:T(2,128)S(1)} %shard_map.73.after_ref.turns_ref, f32[8,9,4,128]{3,2,1,0:T(4,128)S(1)} %all_to_all.10.parts_ref, bf16[2,2048,128]{2,1,0:T(8,128)(2,1)S(1)} %bitcast.10, bf16[2,2048,128]{2,1,0:T(8,128)(2,1)S(1)} %bitcast.11), custom_call_target="tpu_custom_call" | custom-call | flops 7000000000 | bytes 2097152 | tf_op jit(solution)/shard_map/pallas_call | solution.py:216
  23.5 9.5 %all_to_all.11 = bf16[8,32,128]{2,1,0:T(8,128)(2,1)S(1)} all-to-all(bf16[8,32,128]{2,1,0:T(8,128)(2,1)S(1)} %shard_map.75), channel_id=1, replica_groups=mesh['grp'=2,'wide'=8,'narrow'=2] {'wide'}, dimensions={0} | all-to-all | bytes 131072 | tf_op jit(solution)/shard_map/all_to_all | solution.py:226
  33.0 0.0 slice-done
  33.0 0.0 slice-done.1
  33.0 0.0 slice-done.2
  33.0 0.0 slice-done.3
  33.1 2.4 %shard_map.76 = (f32[4,2048]{1,0:T(4,128)S(1)}, f32[4,2048]{1,0:T(4,128)S(1)}) custom-call(s32[1]{0:T(128)} %bitcast.core_ref, bf16[256,128]{1,0:T(8,128)(2,1)S(1)} %bitcast.8, bf16[4096,2048]{1,0:T(8,128)(2,1)S(1)} %bitcast.7), custom_call_target="tpu_custom_call" | custom-call | flops 134217728 | bytes 16777216 | tf_op jit(solution)/shard_map/pallas_call | solution.py:227
  35.4 0.0 collective-permute-start.1
  35.4 1.2 %collective-permute-done.1 = f32[4,2048]{1,0:T(4,128)S(1)} collective-permute-done((f32[4,2048]{1,0:T(4,128)S(1)}, f32[4,2048]{1,0:T(4,128)S(1)}, u32[]{:S(2)}, u32[]{:S(2)}) %collective-permute-start.1) | collective-permute-done | bytes 32800 | tf_op jit(solution)/shard_map/ppermute | solution.py:237
  36.7 0.6 %add_convert_fusion = bf16[4,2048]{1,0:T(4,128)(2,1)} fusion(f32[4,2048]{1,0:T(4,128)S(1)} %get-tuple-element.7, f32[4,2048]{1,0:T(4,128)S(1)} %collective-permute-done.1), kind=kLoop, calls=%fused_computation | loop fusion | flops 16384 | bytes 81920 | tf_op jit(solution)/shard_map/convert_element_type | solution.py:237
  (1 shorter events, 0.0 us)
Async XLA Ops:
  0.0 1.6 %copy-start = (bf16[2048,2,2,128]{3,2,1,0:T(2,128)(2,1)S(1)}, bf16[2048,2,2,128]{3,2,1,0:T(2,128)(2,1)}, u32[]{:S(2)}) copy-start(bf16[2048,2,2,128]{3,2,1,0:T(2,128)(2,1)} %param.9) | copy-start | bytes 6291460
  0.0 1.5 %collective-permute-start = (bf16[4,2048]{1,0:T(4,128)(2,1)}, bf16[4,2048]{1,0:T(4,128)(2,1)S(1)}, u32[]{:S(2)}, u32[]{:S(2)}) collective-permute-start(bf16[4,2048]{1,0:T(4,128)(2,1)} %own_hbm.1), channel_id=1, source_target_pairs={{0,1},{1,0},{2,3},{3,2},{4,5},{5,4},{6,7},{7,6},{8,9},{9,8},{10,11... | collective-permute-start | bytes 49160 | tf_op jit(solution)/shard_map/ppermute | solution.py:196
  1.4 21.3 %copy-start.1 = (bf16[1,2,2048,128]{3,2,1,0:T(8,128)(2,1)S(1)}, bf16[1,2,2048,128]{3,2,1,0:T(8,128)(2,1)}, u32[]{:S(2)}) copy-start(bf16[1,2,2048,128]{3,2,1,0:T(8,128)(2,1)} %param.10) | copy-start | bytes 3145732
  1.4 21.3 %copy-start.2 = (bf16[1,2,2048,128]{3,2,1,0:T(8,128)(2,1)S(1)}, bf16[1,2,2048,128]{3,2,1,0:T(8,128)(2,1)}, u32[]{:S(2)}) copy-start(bf16[1,2,2048,128]{3,2,1,0:T(8,128)(2,1)} %param.11) | copy-start | bytes 3145732
  1.6 31.4 %slice-start = ((s8[16777216]{0:T(1024)(128)(4,1)}), s8[4194304]{0:T(1024)(128)(4,1)S(1)}, s32[]{:S(2)}) async-start(s8[16777216]{0:T(1024)(128)(4,1)} %bitcast.6), calls=%async_computation.2 | async-start | bytes 8388608
  1.6 31.4 %slice-start.1 = ((s8[16777216]{0:T(1024)(128)(4,1)}), s8[4194304]{0:T(1024)(128)(4,1)S(1)}, s32[]{:S(2)}) async-start(s8[16777216]{0:T(1024)(128)(4,1)} %bitcast.6), calls=%async_computation.3 | async-start | bytes 8388608
  7.9 25.2 %slice-start.2 = ((s8[16777216]{0:T(1024)(128)(4,1)}), s8[4194304]{0:T(1024)(128)(4,1)S(1)}, s32[]{:S(2)}) async-start(s8[16777216]{0:T(1024)(128)(4,1)} %bitcast.6), calls=%async_computation.4 | async-start | bytes 8388608
  22.7 10.4 %slice-start.3 = ((s8[16777216]{0:T(1024)(128)(4,1)}), s8[4194304]{0:T(1024)(128)(4,1)S(1)}, s32[]{:S(2)}) async-start(s8[16777216]{0:T(1024)(128)(4,1)} %bitcast.6), calls=%async_computation.5 | async-start | bytes 8388608
  35.4 1.2 %collective-permute-start.1 = (f32[4,2048]{1,0:T(4,128)S(1)}, f32[4,2048]{1,0:T(4,128)S(1)}, u32[]{:S(2)}, u32[]{:S(2)}) collective-permute-start(f32[4,2048]{1,0:T(4,128)S(1)} %get-tuple-element.8), channel_id=1, source_target_pairs={{0,1},{1,0},{2,3},{3,2},{4,5},{5,4},{6,7},{7,6},{8,9},{9,8},{10,11... | collective-permute-start | bytes 98312 | tf_op jit(solution)/shard_map/ppermute | solution.py:237
